TPU v7x, 128 devices: a whole 4x4x4 slice. The times are simulated.
128 devices in a mesh: ctx: 64 (over z, y, x_hi, core), heads: 2 (over x_lo).
Axes of the slice: x: 4 (x_hi: 2, x_lo: 2; x = x_hi * 2 + x_lo), y: 4, z: 4, core: 2. Of those that a mesh axis runs over, the one named last changes fastest.
Arguments:
- hidden: bfloat16 [8192, 768], P('ctx'), may hold values from -6 to 6
- w_qkv: bfloat16 [3, 768, 768], P(None, 'ctx', 'heads'), may hold values from -0.21875 to 0.21875
- w_out: bfloat16 [768, 768], P('heads', 'ctx'), may hold values from -0.875 to 0.875
- b_qv: bfloat16 [2, 768], P(None, 'heads'), may hold values from -3 to 3
- w_up: bfloat16 [768, 3072], P('ctx', 'heads'), may hold values from -0.21875 to 0.21875
- w_down: bfloat16 [3072, 768], P('heads', 'ctx'), may hold values from -0.109375 to 0.109375
- b_up: bfloat16 [3072], P('heads'), may hold values from -3 to 3
- norm_gains: bfloat16 [2, 768], replicated, may hold values from 0.5 to 1.5
- norm_shifts: bfloat16 [4, 768], replicated, may hold values from -3 to 3
- segments: int32 [8192], P('ctx'), may hold values from 0 to 2, as said below
- lengths: int32 [3], replicated, may hold values from 1 to 8192, as said below
- cotangent: bfloat16 [8192, 768], P('ctx'), may hold values from -6 to 6
Outputs:
- layer_out: bfloat16 [8192, 768], P('ctx')
- hidden_grad: float32 [8192, 768], P('ctx')
- qkv_grad: float32 [3, 768, 768], P(None, 'ctx', 'heads')
- out_grad: float32 [768, 768], P('heads', 'ctx')
- qv_grad: float32 [2, 768], P(None, ('heads', 'ctx'))
- up_grad: float32 [768, 3072], P('ctx', 'heads')
- down_grad: float32 [3072, 768], P('heads', 'ctx')
- upbias_grad: float32 [3072], P(('heads', 'ctx'))
- gains_grad: float32 [2, 768], P(None, ('ctx', 'heads'))
- shifts_grad: float32 [4, 768], P(None, ('ctx', 'heads'))
Inputs may be any that keep to these rules, and one draw needn't show every extreme that they name: segments never fall along the tokens and take every value from 0 to 2; each run of equal values is one sequence; one sequence, drawn from the seed, holds all but fewer than 128 of the tokens. lengths[j] counts the leading tokens of sequence j that are not padding, at most the sequence's tokens; fewer than 32 tokens of a sequence are padding.
All inputs are finite; a program needn't handle non-finite values.
Results may differ from a plain program's by a relative error of at most 0.03.
Values may be sent and summed in bfloat16 or wider, within the bound.
No kernel may reach another device: no remote copies, remote signals or barrier semaphores. Data moves between devices by JAX's collectives and lax.ppermute only.
A program may use at most 192 MiB of HBM per device.

v0:
```python
import jax
import jax.numpy as jnp
from jax import lax
from jax.sharding import PartitionSpec as P

HEAD_DIM = 64


EPS = 1e-06
NEG = -1e30


def turned_gather(arrays, axis, dims):
    turned = [jnp.moveaxis(a, dim, 0) for a, dim in zip(arrays, dims)]
    widths = [t[0].size for t in turned]
    both = jnp.concatenate([t.reshape(-1, w) for t, w in zip(turned, widths)], axis=1)
    result = lax.all_gather(both, axis, axis=0, tiled=True)
    blocks = jnp.split(result, [sum(widths[:k]) for k in range(1, len(widths))], axis=1)
    return tuple(
        (
            jnp.moveaxis(b.reshape(-1, *t.shape[1:]), 0, dim)
            for b, t, dim in zip(blocks, turned, dims)
        )
    )


def copy_for_each(x, axis):
    peers = lax.axis_size(axis)
    return lax.all_to_all(jnp.broadcast_to(x[None], (peers, *x.shape)), axis, 0, 0, tiled=True)


def over_copies(x, axis):
    everything = copy_for_each(x, axis)
    return jnp.sum(everything, axis=0)


def sent_together(arrays, axis, dim, along):
    columns = [a.reshape(*a.shape[:along], -1) for a in arrays]
    both = jnp.concatenate(columns, axis=along)
    result, at, done = (lax.all_gather(both, axis, axis=dim, tiled=True), 0, [])
    for a, column in zip(arrays, columns):
        section = result[..., at : at + column.shape[along]]
        done.append(section.reshape(*section.shape[:along], *a.shape[along:]))
        at += column.shape[along]
    return tuple(done)


def of_everyone(x, axis):
    everything = copy_for_each(x, axis)
    return jnp.sum(everything.astype(jnp.float32), axis=0)


def in_one_piece(arrays, axis, dim, along):
    both = jnp.concatenate(arrays, axis=along)
    result, at, done = (lax.psum_scatter(both, axis, scatter_dimension=dim, tiled=True), 0, [])
    for a in arrays:
        done.append(lax.slice_in_dim(result, at, at + a.shape[along], axis=along))
        at += a.shape[along]
    return tuple(done)


def layer_norm(residual, gain_row, shift_row):
    centred = residual - jnp.mean(residual, axis=-1, keepdims=True)
    inverse = lax.rsqrt(jnp.mean(centred * centred, axis=-1, keepdims=True) + EPS)
    normed = centred * inverse
    return (normed * gain_row + shift_row, normed, inverse)


def norm_back(incoming, normed, inverse, gain_row):
    scaled = incoming * gain_row
    projected = (
        scaled
        - jnp.mean(scaled, axis=-1, keepdims=True)
        - normed * jnp.mean(scaled * normed, axis=-1, keepdims=True)
    )
    return (inverse * projected, jnp.sum(incoming * normed, axis=0), jnp.sum(incoming, axis=0))


def exact_gelu(pre_act):
    return jax.nn.gelu(pre_act, approximate=False)


def per_device(
    hidden,
    w_qkv,
    w_out,
    b_qv,
    w_up,
    w_down,
    b_up,
    norm_gains,
    norm_shifts,
    segments,
    lengths,
    cotangent,
):
    cycle_index = lax.axis_index("ctx")
    head_index = lax.axis_index("heads")
    tok_rows = hidden.shape[0]
    qkv_all, out_all, up_all, down_all = turned_gather(
        (w_qkv, w_out, w_up, w_down), "ctx", (1, 1, 0, 1)
    )
    head_width = qkv_all.shape[2]
    head_count = head_width // HEAD_DIM
    score_scale = HEAD_DIM ** (-0.5)
    seq_index = jnp.arange(lengths.shape[0], dtype=jnp.int32)
    member = (segments[:, None] == seq_index[None, :]).astype(jnp.int32)
    totals = over_copies(jnp.sum(member, axis=0), "ctx")
    starts = jnp.cumsum(totals) - totals
    local_rows = jnp.arange(tok_rows, dtype=jnp.int32)
    places = cycle_index * tok_rows + local_rows
    run_start = jnp.sum(member * starts[None, :], axis=1)
    run_valid = jnp.sum(member * lengths[None, :], axis=1)
    key_tag = jnp.where(places - run_start < run_valid, segments, -1).astype(jnp.bfloat16)
    query_tag = segments.astype(jnp.bfloat16)
    queries = (
        jnp.dot(hidden, qkv_all[0], preferred_element_type=jnp.float32)
        + b_qv[0].astype(jnp.float32)
    ).astype(jnp.bfloat16)
    keys_low = jnp.dot(hidden, qkv_all[1], preferred_element_type=jnp.float32).astype(jnp.bfloat16)
    values_low = (
        jnp.dot(hidden, qkv_all[2], preferred_element_type=jnp.float32)
        + b_qv[1].astype(jnp.float32)
    ).astype(jnp.bfloat16)
    query_heads = queries.reshape(tok_rows, head_count, HEAD_DIM)

    def block_scores(q_heads, q_tag, q_places, key_block, tag_block):
        key_count = key_block.shape[0]
        key_heads = key_block.reshape(key_count, head_count, HEAD_DIM)
        scores = (
            jnp.einsum("qhd,khd->hqk", q_heads, key_heads, preferred_element_type=jnp.float32)
            * score_scale
        )
        key_places = jnp.arange(key_count, dtype=jnp.int32)
        allowed = (q_tag[:, None] == tag_block[None, :]) | (
            q_places[:, None] == key_places[None, :]
        )
        return (jnp.where(allowed[None], scores, NEG), key_heads)

    running_max = jnp.full((head_count, tok_rows), NEG, jnp.float32)
    key_block, value_block, tag_block = sent_together((keys_low, values_low, key_tag), "ctx", 0, 1)
    scores, key_heads = block_scores(query_heads, query_tag, places, key_block, tag_block)
    value_heads = value_block.reshape(key_block.shape[0], head_count, HEAD_DIM)
    new_max = jnp.maximum(running_max, jnp.max(scores, axis=-1))
    weights = jnp.exp(scores - new_max[:, :, None])
    new_sum = jnp.sum(weights, axis=-1)
    update = jnp.einsum(
        "hqk,khd->qhd",
        weights.astype(jnp.bfloat16),
        value_heads,
        preferred_element_type=jnp.float32,
    )
    attended = update / jnp.transpose(new_sum)[:, :, None]
    attended_low = attended.reshape(tok_rows, head_width).astype(jnp.bfloat16)
    attn_mixed = of_everyone(
        jnp.dot(attended_low, out_all, preferred_element_type=jnp.float32).astype(jnp.bfloat16),
        "heads",
    ).astype(jnp.float32)
    gain_rows = norm_gains.astype(jnp.float32)
    shifts = norm_shifts.astype(jnp.float32)
    first_out, normed_one, inverse_one = layer_norm(
        hidden.astype(jnp.float32) + attn_mixed + shifts[0], gain_rows[0], shifts[1]
    )
    first_low = first_out.astype(jnp.bfloat16)
    up_proj = jnp.dot(first_low, up_all, preferred_element_type=jnp.float32) + b_up.astype(
        jnp.float32
    )
    activated = exact_gelu(up_proj).astype(jnp.bfloat16)
    second = of_everyone(
        jnp.dot(activated, down_all, preferred_element_type=jnp.float32).astype(jnp.bfloat16),
        "heads",
    ).astype(jnp.float32)
    output, normed_two, inverse_two = layer_norm(
        first_out + second + shifts[2], gain_rows[1], shifts[3]
    )
    resid_two, gain_two_grad, beta_two_grad = norm_back(
        cotangent.astype(jnp.float32), normed_two, inverse_two, gain_rows[1]
    )
    branch_low = resid_two.astype(jnp.bfloat16)
    down_grad = jnp.einsum("tf,td->fd", activated, branch_low, preferred_element_type=jnp.float32)
    act_grad = jnp.einsum("td,fd->tf", branch_low, down_all, preferred_element_type=jnp.float32)
    gelu_pull = jax.vjp(exact_gelu, up_proj)[1]
    up_low = gelu_pull(act_grad)[0].astype(jnp.bfloat16)
    up_grad = jnp.einsum("td,tf->df", first_low, up_low, preferred_element_type=jnp.float32)
    upbias_grad = jnp.sum(up_low.astype(jnp.float32), axis=0)
    first_grad = resid_two + of_everyone(
        jnp.einsum("tf,df->td", up_low, up_all, preferred_element_type=jnp.float32).astype(
            jnp.bfloat16
        ),
        "heads",
    ).astype(jnp.float32)
    resid_one, gain_one_grad, beta_one_grad = norm_back(
        first_grad, normed_one, inverse_one, gain_rows[0]
    )
    mixed_low = resid_one.astype(jnp.bfloat16)
    out_grad = jnp.einsum("th,td->hd", attended_low, mixed_low, preferred_element_type=jnp.float32)
    attended_grad = jnp.einsum(
        "td,hd->th", mixed_low, out_all, preferred_element_type=jnp.float32
    ).astype(jnp.bfloat16)
    grad_heads = attended_grad.reshape(tok_rows, head_count, HEAD_DIM)
    row_delta = jnp.sum(grad_heads.astype(jnp.float32) * attended, axis=-1)
    key_block, value_block, tag_block = sent_together((keys_low, values_low, key_tag), "ctx", 0, 1)
    scores, key_heads = block_scores(query_heads, query_tag, places, key_block, tag_block)
    key_count = key_block.shape[0]
    value_heads = value_block.reshape(key_count, head_count, HEAD_DIM)
    prob_rows = jnp.exp(scores - new_max[:, :, None]) / new_sum[:, :, None]
    prob_grad = jnp.einsum(
        "qhd,khd->hqk", grad_heads, value_heads, preferred_element_type=jnp.float32
    )
    score_grad = (prob_rows * (prob_grad - jnp.transpose(row_delta)[:, :, None])).astype(
        jnp.bfloat16
    )
    value_part = jnp.einsum(
        "hqk,qhd->khd",
        prob_rows.astype(jnp.bfloat16),
        grad_heads,
        preferred_element_type=jnp.float32,
    )
    key_part = (
        jnp.einsum("hqk,qhd->khd", score_grad, query_heads, preferred_element_type=jnp.float32)
        * score_scale
    )
    query_part = (
        jnp.einsum("hqk,khd->qhd", score_grad, key_heads, preferred_element_type=jnp.float32)
        * score_scale
    )
    key_part, value_part, query_part = (
        key_part.reshape(key_count, head_width),
        value_part.reshape(key_count, head_width),
        query_part,
    )
    key_count = key_block.shape[0]
    key_grad, value_grad = in_one_piece((key_part, value_part), "ctx", 0, 1)
    query_low = query_part.reshape(tok_rows, head_width).astype(jnp.bfloat16)
    key_low_grad = key_grad.astype(jnp.bfloat16)
    value_low_grad = value_grad.astype(jnp.bfloat16)
    qkv_grad = jnp.stack(
        [
            jnp.einsum("td,th->dh", hidden, member_grad, preferred_element_type=jnp.float32)
            for member_grad in (query_low, key_low_grad, value_low_grad)
        ]
    )
    qv_grad = jnp.stack(
        [
            jnp.sum(query_low.astype(jnp.float32), axis=0),
            jnp.sum(value_low_grad.astype(jnp.float32), axis=0),
        ]
    )
    spread = jnp.einsum("th,dh->td", query_low, qkv_all[0], preferred_element_type=jnp.float32)
    spread = spread + jnp.einsum(
        "th,dh->td", key_low_grad, qkv_all[1], preferred_element_type=jnp.float32
    )
    spread = spread + jnp.einsum(
        "th,dh->td", value_low_grad, qkv_all[2], preferred_element_type=jnp.float32
    )
    hidden_grad = resid_one + of_everyone(spread.astype(jnp.bfloat16), "heads").astype(jnp.float32)
    vectors = jnp.stack(
        [
            gain_one_grad,
            gain_two_grad,
            jnp.sum(resid_one, axis=0),
            beta_one_grad,
            jnp.sum(resid_two, axis=0),
            beta_two_grad,
        ]
    )
    reduced = (
        lax.psum_scatter(qkv_grad, "ctx", scatter_dimension=1, tiled=True),
        lax.psum_scatter(out_grad, "ctx", scatter_dimension=1, tiled=True),
        lax.psum_scatter(up_grad, "ctx", scatter_dimension=0, tiled=True),
        lax.psum_scatter(down_grad, "ctx", scatter_dimension=1, tiled=True),
        lax.psum_scatter(qv_grad, "ctx", scatter_dimension=1, tiled=True),
        lax.psum_scatter(upbias_grad, "ctx", scatter_dimension=0, tiled=True),
        lax.psum_scatter(vectors, "ctx", scatter_dimension=1, tiled=True),
    )
    share_width = reduced[6].shape[1] // lax.axis_size("heads")
    own_part = lax.dynamic_slice_in_dim(reduced[6], head_index * share_width, share_width, 1)
    return (
        output.astype(jnp.bfloat16),
        hidden_grad,
        reduced[0],
        reduced[1],
        reduced[4],
        reduced[2],
        reduced[3],
        reduced[5],
        own_part[:2],
        own_part[2:],
    )


def solution(mesh):
    placed = (
        P("ctx", None),
        P(None, "ctx", "heads"),
        P("heads", "ctx"),
        P(None, "heads"),
        P("ctx", "heads"),
        P("heads", "ctx"),
        P("heads"),
        P(),
        P(),
        P("ctx"),
        P(),
        P("ctx", None),
    )
    return jax.shard_map(
        per_device,
        mesh=mesh,
        in_specs=placed,
        out_specs=(
            P("ctx", None),
            P("ctx", None),
            P(None, "ctx", "heads"),
            P("heads", "ctx"),
            P(None, ("heads", "ctx")),
            P("ctx", "heads"),
            P("heads", "ctx"),
            P(("heads", "ctx")),
            P(None, ("ctx", "heads")),
            P(None, ("ctx", "heads")),
        ),
        check_vma=False,
    )
```

profile of v0, /device:TPU:1, one launch (start us, length us, event | category | flops | bytes accessed | tf_op | source)
XLA Modules:
  0.0 1384.8 jit_solution(14171654898203138469)
XLA Ops:
  11.0 12.5 all-to-all-start
  24.9 7.8 all-to-all-done
  35.0 65.0 %all-gather.6.cloned.1.call-done = bf16[64,12,4608]{2,1,0:T(8,128)(2,1)} async-done(((bf16[1,12,4608]{2,1,0:T(8,128)(2,1)}), bf16[64,12,4608]{2,1,0:T(8,128)(2,1)}) %all-gather.6.cloned.1.call-update) | async-done | bytes 7077904 | tf_op jit(solution)/shard_map/all_gather | solution.py:17
  99.9 10.7 reshape.213
  118.7 113.6 %all-gather.4.cloned.1.call-done = bf16[8192,769]{0,1:T(8,128)(2,1)} async-done(((bf16[128,769]{0,1:T(8,128)(2,1)}), bf16[8192,769]{0,1:T(8,128)(2,1)}) %all-gather.4.cloned.1.call-update) | async-done | bytes 12599312 | tf_op jit(solution)/shard_map/all_gather | solution.py:40
  234.7 8.1 fusion.83
  242.8 10.7 fusion.3
  253.6 11.8 fusion.5
  265.4 13.5 fusion.86
  285.1 6.0 all-to-all-done.1
  296.4 7.9 all_to_all.26
  311.0 7.1 all_to_all.27
  320.1 15.5 %fusion.7 = f32[6,64,8192]{2,1,0:T(8,128)} fusion(bf16[128,6,64]{0,2,1:T(8,128)(2,1)S(1)} %bitcast.129, f32[6,128,8192]{2,1,0:T(8,128)} %get-tuple-element.114, f32[6,128]{1,0:T(8,128)S(1)} %fusion.5, f32[6,128]{1,0:T(8,128)S(1)} %broadcast_maximum_fusion, pred[128,8192]{1,0:T(8,128)(4,1)S(1)} %fusion.12), kind=kOutput, calls=%fused_computation.8 | convolution fusion | flops 836763648 | bytes 38901760 | tf_op jit(solution)/shard_map/hqk,qhd->khd/dot_general | solution.py:213
  335.7 18.9 %multiply_convert_fusion = bf16[6,128,8192]{2,1,0:T(8,128)(2,1)} fusion(bf16[128,6,64]{0,2,1:T(8,128)(2,1)S(1)} %bitcast.131, bf16[8192,6,64]{0,2,1:T(8,128)(2,1)} %bitcast.122, f32[6,128]{1,0:T(8,128)S(1)} %bitcast.138, f32[6,128]{1,0:T(8,128)S(1)} %fusion.5, f32[6,128]{1,0:T(8,128)S(1)} %broadcast_maximum_fusion, f32[6,128,8192]{2,1,0:T(8,128)} %get-tuple-element.114, ...), kind=kOutput, calls=%fused_computation.1 | convolution fusion | flops 849346560 | bytes 45196288 | tf_op jit(solution)/shard_map/qhd,khd->hqk/dot_general | solution.py:207
  354.6 5.7 convolution_multiply_fusion
  360.2 15.8 %pad_maximum_fusion = f32[8192,768]{0,1:T(8,128)} fusion(f32[8192,384]{0,1:T(8,128)} %bitcast.114, f32[8192,384]{0,1:T(8,128)S(1)} %bitcast.111), kind=kLoop, calls=%fused_computation | loop fusion | flops 6291456 | bytes 50331648 | tf_op jit(solution)/shard_map/concatenate | solution.py:54
  382.4 12.4 convert_reduce_fusion.7
  397.6 213.4 %reduce-scatter.10.cloned.1.call-done = f32[128,768]{0,1:T(8,128)} async-done(((f32[8192,768]{0,1:T(8,128)}), f32[128,768]{0,1:T(8,128)}) %reduce-scatter.10.cloned.1.call-update) | async-done | bytes 393232 | tf_op jit(solution)/shard_map/reduce_scatter | solution.py:55
  618.6 204.5 %fusion.77 = (f32[384,16]{0,1:T(8,128)S(1)}, f32[16,1536]{1,0:T(8,128)S(1)}, f32[1536,16]{0,1:T(8,128)S(1)}) fusion(f32[384,768]{0,1:T(8,128)} %fusion.58, f32[768,1536]{1,0:T(8,128)} %fusion.74, f32[1536,768]{0,1:T(8,128)} %fusion.61), kind=kCustom, calls=%all-reduce-scatter.3 | all-reduce-scatter fusion | flops 3538945 | bytes 10838528
  831.1 16.8 %collective-permute-start.9 = (f32[384,16]{0,1:T(8,128)S(1)}, f32[384,16]{0,1:T(8,128)S(1)}, u32[]{:S(2)}, u32[]{:S(2)}) collective-permute-start(f32[384,16]{0,1:T(8,128)S(1)} %get-tuple-element.94), channel_id=1, source_target_pairs={{0,20},{2,22},{4,24},{6,26},{8,28},{10,30},{12,32},{14,34},{16,36}... | collective-permute-start | bytes 73736
  848.0 4.3 collective-permute-start.8
  861.5 6.9 collective-permute-start.4
  872.0 4.4 collective-permute-start.1
  876.4 5.1 collective-permute-start
  902.9 10.7 collective-permute-start.21
  916.3 4.9 collective-permute-start.18
  925.3 5.2 collective-permute-start.16
  962.3 12.4 concatenate.13
  974.8 5.5 collective-permute-start.36
  992.1 27.5 %concatenate.14 = f32[268,1536]{1,0:T(8,128)} concatenate(f32[12,1536]{1,0:T(8,128)} %copy-done.16, f32[16,1536]{1,0:T(8,128)} %copy-done.17, f32[16,1536]{1,0:T(8,128)} %copy-done.18, f32[16,1536]{1,0:T(8,128)} %copy-done.19, f32[16,1536]{1,0:T(8,128)} %copy-done.20, f32[16,1536]{1,0:T(8,128)} %copy-done.21, f32[16,1536]{1,0:T(8,128)} %copy-done.22, f32[16,1536]{1,0:T(8,128)} %copy-done.23, ...), dimensions={0} | concatenate | bytes 3293184
  1019.6 26.5 %concatenate.15 = f32[1536,268]{0,1:T(8,128)} concatenate(f32[1536,12]{0,1:T(8,128)S(1)} %collective-permute-done.47, f32[1536,16]{0,1:T(8,128)} %collective-permute-done.46, f32[1536,16]{0,1:T(8,128)} %collective-permute-done.45, f32[1536,16]{0,1:T(8,128)} %collective-permute-done.44, f32[1536,16]{0,1:T(8,128)} %collective-permute-done.43, f32[1536,16]{0,1:T(8,128)} %collective-permute-done.42, ...), dimensions={1} | concatenate | bytes 3293184
  1054.2 319.0 %all-reduce.10 = (f32[2,384]{1,0:T(2,128)S(1)}, f32[1536]{0:T(1024)S(1)}, f32[6,768]{1,0:T(8,128)S(1)}) all-reduce(f32[2,384]{1,0:T(2,128)S(1)} %pad_maximum_fusion.3, f32[1536]{0:T(1024)S(1)} %copy-done.49, f32[6,768]{1,0:T(8,128)S(1)} %stack.55), channel_id=5, replica_groups=mesh['ctx'=64,'heads'=2] {'ctx'}, use_global_device_ids=true, to_apply=%region_25.26.clone | all-reduce | flops 6912 | bytes 55296
  (308 shorter events, 156.5 us)
Async XLA Ops:
  7.2 92.8 %all-gather.6.cloned.1.call-start = ((), (), s32[]{:S(2)}) async-start(), calls=%async_computation.8 | async-start | bytes 9584640 | tf_op jit(solution)/shard_map/all_gather | solution.py:17
  11.0 21.7 %all-to-all-start = ((s32[64,1,3]{2,1,0:T(1,128)}), s32[64,1,3]{2,1,0:T(1,128)S(1)}, u32[]{:S(2)}, u32[]{:S(2)}) async-start(s32[64,1,3]{2,1,0:T(1,128)} %broadcast_in_dim.32), calls=%async_computation | async-start | bytes 65536 | tf_op jit(solution)/shard_map/all_to_all | solution.py:29
  23.5 208.8 %all-gather.4.cloned.1.call-start = ((), (), s32[]{:S(2)}) async-start(), calls=%async_computation.6 | async-start | bytes 12912640 | tf_op jit(solution)/shard_map/all_gather | solution.py:40
  284.7 326.4 %reduce-scatter.10.cloned.1.call-start = ((), (), s32[]{:S(2)}) async-start(), calls=%async_computation.7 | async-start | bytes 25559040 | tf_op jit(solution)/shard_map/reduce_scatter | solution.py:55
  376.1 1000.4 %all-reduce.14.cloned.1.call-start = ((), (), s32[]{:S(2)}) async-start(), calls=%async_computation.9 | async-start | bytes 9437184
  825.9 22.1 %collective-permute-start.13 = (f32[384,16]{0,1:T(8,128)S(1)}, f32[384,16]{0,1:T(8,128)S(1)}, u32[]{:S(2)}, u32[]{:S(2)}) collective-permute-start(f32[384,16]{0,1:T(8,128)S(1)} %get-tuple-element.94), channel_id=1, source_target_pairs={{0,28},{2,30},{4,32},{6,34},{8,36},{10,38},{12,40},{14,42},{16,44}... | collective-permute-start | bytes 73736
  827.2 25.2 %collective-permute-start.12 = (f32[384,16]{0,1:T(8,128)S(1)}, f32[384,16]{0,1:T(8,128)S(1)}, u32[]{:S(2)}, u32[]{:S(2)}) collective-permute-start(f32[384,16]{0,1:T(8,128)S(1)} %get-tuple-element.94), channel_id=1, source_target_pairs={{0,26},{2,28},{4,30},{6,32},{8,34},{10,36},{12,38},{14,40},{16,42}... | collective-permute-start | bytes 73736
  828.5 25.2 %collective-permute-start.11 = (f32[384,16]{0,1:T(8,128)S(1)}, f32[384,16]{0,1:T(8,128)S(1)}, u32[]{:S(2)}, u32[]{:S(2)}) collective-permute-start(f32[384,16]{0,1:T(8,128)S(1)} %get-tuple-element.94), channel_id=1, source_target_pairs={{0,24},{2,26},{4,28},{6,30},{8,32},{10,34},{12,36},{14,38},{16,40}... | collective-permute-start | bytes 73736
  829.8 26.7 %collective-permute-start.10 = (f32[384,16]{0,1:T(8,128)S(1)}, f32[384,16]{0,1:T(8,128)S(1)}, u32[]{:S(2)}, u32[]{:S(2)}) collective-permute-start(f32[384,16]{0,1:T(8,128)S(1)} %get-tuple-element.94), channel_id=1, source_target_pairs={{0,22},{2,24},{4,26},{6,28},{8,30},{10,32},{12,34},{14,36},{16,38}... | collective-permute-start | bytes 73736
  831.1 26.8 %collective-permute-start.9 = (f32[384,16]{0,1:T(8,128)S(1)}, f32[384,16]{0,1:T(8,128)S(1)}, u32[]{:S(2)}, u32[]{:S(2)}) collective-permute-start(f32[384,16]{0,1:T(8,128)S(1)} %get-tuple-element.94), channel_id=1, source_target_pairs={{0,20},{2,22},{4,24},{6,26},{8,28},{10,30},{12,32},{14,34},{16,36}... | collective-permute-start | bytes 73736
  856.5 33.0 %collective-permute-start.31 = (f32[12,1536]{1,0:T(8,128)S(1)}, f32[12,1536]{1,0:T(8,128)S(1)}, u32[]{:S(2)}, u32[]{:S(2)}) collective-permute-start(f32[12,1536]{1,0:T(8,128)S(1)} %slice.97), channel_id=1, source_target_pairs={{0,32},{2,34},{4,36},{6,38},{8,40},{10,42},{12,44},{14,46},{16,48}... | collective-permute-start | bytes 221192
  857.9 33.0 %collective-permute-start.47 = (f32[1536,12]{0,1:T(8,128)S(1)}, f32[1536,12]{0,1:T(8,128)S(1)}, u32[]{:S(2)}, u32[]{:S(2)}) collective-permute-start(f32[1536,12]{0,1:T(8,128)S(1)} %slice.98), channel_id=1, source_target_pairs={{0,32},{2,34},{4,36},{6,38},{8,40},{10,42},{12,44},{14,46},{16,48}... | collective-permute-start | bytes 221192
  892.2 21.4 %collective-permute-start.25 = (f32[16,1536]{1,0:T(8,128)S(1)}, f32[16,1536]{1,0:T(8,128)S(1)}, u32[]{:S(2)}, u32[]{:S(2)}) collective-permute-start(f32[16,1536]{1,0:T(8,128)S(1)} %get-tuple-element.95), channel_id=1, source_target_pairs={{0,20},{2,22},{4,24},{6,26},{8,28},{10,30},{12,32},{14,34},{16,36}... | collective-permute-start | bytes 294920
  893.6 21.4 %collective-permute-start.24 = (f32[16,1536]{1,0:T(8,128)S(1)}, f32[16,1536]{1,0:T(8,128)S(1)}, u32[]{:S(2)}, u32[]{:S(2)}) collective-permute-start(f32[16,1536]{1,0:T(8,128)S(1)} %get-tuple-element.95), channel_id=1, source_target_pairs={{0,18},{2,20},{4,22},{6,24},{8,26},{10,28},{12,30},{14,32},{16,34}... | collective-permute-start | bytes 294920
  897.5 18.8 %collective-permute-start.23 = (f32[16,1536]{1,0:T(8,128)S(1)}, f32[16,1536]{1,0:T(8,128)S(1)}, u32[]{:S(2)}, u32[]{:S(2)}) collective-permute-start(f32[16,1536]{1,0:T(8,128)S(1)} %get-tuple-element.95), channel_id=1, source_target_pairs={{0,16},{2,18},{4,20},{6,22},{8,24},{10,26},{12,28},{14,30},{16,32}... | collective-permute-start | bytes 294920
  900.8 20.4 %collective-permute-start.22 = (f32[16,1536]{1,0:T(8,128)S(1)}, f32[16,1536]{1,0:T(8,128)S(1)}, u32[]{:S(2)}, u32[]{:S(2)}) collective-permute-start(f32[16,1536]{1,0:T(8,128)S(1)} %get-tuple-element.95), channel_id=1, source_target_pairs={{0,14},{2,16},{4,18},{6,20},{8,22},{10,24},{12,26},{14,28},{16,30}... | collective-permute-start | bytes 294920
  902.9 22.4 %collective-permute-start.21 = (f32[16,1536]{1,0:T(8,128)S(1)}, f32[16,1536]{1,0:T(8,128)S(1)}, u32[]{:S(2)}, u32[]{:S(2)}) collective-permute-start(f32[16,1536]{1,0:T(8,128)S(1)} %get-tuple-element.95), channel_id=1, source_target_pairs={{0,12},{2,14},{4,16},{6,18},{8,20},{10,22},{12,24},{14,26},{16,28}... | collective-permute-start | bytes 294920
  916.3 18.0 %collective-permute-start.18 = (f32[16,1536]{1,0:T(8,128)S(1)}, f32[16,1536]{1,0:T(8,128)S(1)}, u32[]{:S(2)}, u32[]{:S(2)}) collective-permute-start(f32[16,1536]{1,0:T(8,128)S(1)} %get-tuple-element.95), channel_id=1, source_target_pairs={{0,6},{2,8},{4,10},{6,12},{8,14},{10,16},{12,18},{14,20},{16,22},{... | collective-permute-start | bytes 294920
  934.4 19.4 %collective-permute-start.44 = (f32[1536,16]{0,1:T(8,128)S(1)}, f32[1536,16]{0,1:T(8,128)}, u32[]{:S(2)}, u32[]{:S(2)}) collective-permute-start(f32[1536,16]{0,1:T(8,128)S(1)} %get-tuple-element.96), channel_id=1, source_target_pairs={{0,26},{2,28},{4,30},{6,32},{8,34},{10,36},{12,38},{14,40},{16,42}... | collective-permute-start | bytes 294920
  936.3 19.4 %collective-permute-start.43 = (f32[1536,16]{0,1:T(8,128)S(1)}, f32[1536,16]{0,1:T(8,128)}, u32[]{:S(2)}, u32[]{:S(2)}) collective-permute-start(f32[1536,16]{0,1:T(8,128)S(1)} %get-tuple-element.96), channel_id=1, source_target_pairs={{0,24},{2,26},{4,28},{6,30},{8,32},{10,34},{12,36},{14,38},{16,40}... | collective-permute-start | bytes 294920
  938.2 19.4 %collective-permute-start.42 = (f32[1536,16]{0,1:T(8,128)S(1)}, f32[1536,16]{0,1:T(8,128)}, u32[]{:S(2)}, u32[]{:S(2)}) collective-permute-start(f32[1536,16]{0,1:T(8,128)S(1)} %get-tuple-element.96), channel_id=1, source_target_pairs={{0,22},{2,24},{4,26},{6,28},{8,30},{10,32},{12,34},{14,36},{16,38}... | collective-permute-start | bytes 294920
  947.2 27.5 %collective-permute-start.41 = (f32[1536,16]{0,1:T(8,128)S(1)}, f32[1536,16]{0,1:T(8,128)}, u32[]{:S(2)}, u32[]{:S(2)}) collective-permute-start(f32[1536,16]{0,1:T(8,128)S(1)} %get-tuple-element.96), channel_id=1, source_target_pairs={{0,20},{2,22},{4,24},{6,26},{8,28},{10,30},{12,32},{14,34},{16,36}... | collective-permute-start | bytes 294920
  950.3 30.0 %collective-permute-start.40 = (f32[1536,16]{0,1:T(8,128)S(1)}, f32[1536,16]{0,1:T(8,128)}, u32[]{:S(2)}, u32[]{:S(2)}) collective-permute-start(f32[1536,16]{0,1:T(8,128)S(1)} %get-tuple-element.96), channel_id=1, source_target_pairs={{0,18},{2,20},{4,22},{6,24},{8,26},{10,28},{12,30},{14,32},{16,34}... | collective-permute-start | bytes 294920
  953.7 28.5 %collective-permute-start.39 = (f32[1536,16]{0,1:T(8,128)S(1)}, f32[1536,16]{0,1:T(8,128)}, u32[]{:S(2)}, u32[]{:S(2)}) collective-permute-start(f32[1536,16]{0,1:T(8,128)S(1)} %get-tuple-element.96), channel_id=1, source_target_pairs={{0,16},{2,18},{4,20},{6,22},{8,24},{10,26},{12,28},{14,30},{16,32}... | collective-permute-start | bytes 294920
  955.7 28.5 %collective-permute-start.38 = (f32[1536,16]{0,1:T(8,128)S(1)}, f32[1536,16]{0,1:T(8,128)}, u32[]{:S(2)}, u32[]{:S(2)}) collective-permute-start(f32[1536,16]{0,1:T(8,128)S(1)} %get-tuple-element.96), channel_id=1, source_target_pairs={{0,14},{2,16},{4,18},{6,20},{8,22},{10,24},{12,26},{14,28},{16,30}... | collective-permute-start | bytes 294920
  957.6 30.0 %collective-permute-start.37 = (f32[1536,16]{0,1:T(8,128)S(1)}, f32[1536,16]{0,1:T(8,128)}, u32[]{:S(2)}, u32[]{:S(2)}) collective-permute-start(f32[1536,16]{0,1:T(8,128)S(1)} %get-tuple-element.96), channel_id=1, source_target_pairs={{0,12},{2,14},{4,16},{6,18},{8,20},{10,22},{12,24},{14,26},{16,28}... | collective-permute-start | bytes 294920
  974.8 44.8 %collective-permute-start.36 = (f32[1536,16]{0,1:T(8,128)S(1)}, f32[1536,16]{0,1:T(8,128)}, u32[]{:S(2)}, u32[]{:S(2)}) collective-permute-start(f32[1536,16]{0,1:T(8,128)S(1)} %get-tuple-element.96), channel_id=1, source_target_pairs={{0,10},{2,12},{4,14},{6,16},{8,18},{10,20},{12,22},{14,24},{16,26}... | collective-permute-start | bytes 294920
  980.3 39.2 %collective-permute-start.35 = (f32[1536,16]{0,1:T(8,128)S(1)}, f32[1536,16]{0,1:T(8,128)}, u32[]{:S(2)}, u32[]{:S(2)}) collective-permute-start(f32[1536,16]{0,1:T(8,128)S(1)} %get-tuple-element.96), channel_id=1, source_target_pairs={{0,8},{2,10},{4,12},{6,14},{8,16},{10,18},{12,20},{14,22},{16,24},... | collective-permute-start | bytes 294920
  982.2 37.3 %collective-permute-start.34 = (f32[1536,16]{0,1:T(8,128)S(1)}, f32[1536,16]{0,1:T(8,128)}, u32[]{:S(2)}, u32[]{:S(2)}) collective-permute-start(f32[1536,16]{0,1:T(8,128)S(1)} %get-tuple-element.96), channel_id=1, source_target_pairs={{0,6},{2,8},{4,10},{6,12},{8,14},{10,16},{12,18},{14,20},{16,22},{... | collective-permute-start | bytes 294920
  984.2 35.4 %collective-permute-start.33 = (f32[1536,16]{0,1:T(8,128)S(1)}, f32[1536,16]{0,1:T(8,128)}, u32[]{:S(2)}, u32[]{:S(2)}) collective-permute-start(f32[1536,16]{0,1:T(8,128)S(1)} %get-tuple-element.96), channel_id=1, source_target_pairs={{0,4},{2,6},{4,8},{6,10},{8,12},{10,14},{12,16},{14,18},{16,20},{1... | collective-permute-start | bytes 294920
  987.6 31.9 %collective-permute-start.32 = (f32[1536,16]{0,1:T(8,128)S(1)}, f32[1536,16]{0,1:T(8,128)}, u32[]{:S(2)}, u32[]{:S(2)}) collective-permute-start(f32[1536,16]{0,1:T(8,128)S(1)} %get-tuple-element.96), channel_id=1, source_target_pairs={{0,2},{2,4},{4,6},{6,8},{8,10},{10,12},{12,14},{14,16},{16,18},{18... | collective-permute-start | bytes 294920
  1050.6 325.0 %all-to-all-start.4 = ((bf16[2,128,768]{2,1,0:T(8,128)(2,1)}), bf16[2,128,768]{2,1,0:T(8,128)(2,1)S(1)}, u32[]{:S(2)}, u32[]{:S(2)}) async-start(bf16[2,128,768]{2,1,0:T(8,128)(2,1)} %broadcast_in_dim.40), calls=%async_computation.5 | async-start | bytes 786432 | tf_op jit(solution)/shard_map/all_to_all | solution.py:29
  (79 other events, 4840.2 us)
Sparse Core Ops, SparseCore 0:
  11.7 88.2 all-gather.5
  117.4 114.8 all-gather.3
  376.2 234.7 reduce-scatter.9
  618.7 656.5 all-reduce.13
where the time goes:
time: 1410 us; the launch traced here: 1380 us
  blocking collectives  538 us (38%)
  waiting for transfers between devices  406 us (29%)
  starting transfers between devices  165 us (12%)
  local copies, waits for them, and re-layouts  111 us (8%)
  matrix products  101 us (7%)
  other arithmetic  44.6 us (3%)
  between operations  18.1 us (1%)
    unnamed x2, blocking collectives  523 us
    reduce_scatter x1, waiting for transfers between devices, in_one_piece(): lax.psum_scatter(both, axis, scatter_dimension=dim, tiled=True)  213 us
    unnamed x49, starting transfers between devices  146 us
    all_gather x1, waiting for transfers between devices, sent_together(): result, at, done = (lax.all_gather(both, axis, axis=dim, tiled=True), 0, [])  114 us
    unnamed x129, local copies, waits for them, and re-layouts  85.5 us
    all_gather x1, waiting for transfers between devices, turned_gather(): result = lax.all_gather(both, axis, axis=0, tiled=True)  65 us
  transfers between devices with their start and end apart: 55, of which 5 were waited for; matrix products, arithmetic and copies ran while one was open for 23% of the time, Pallas kernels for 0%

commit v1 on v0

v1 whole, which is shorter than its diff:
```python
import jax
import jax.numpy as jnp
from jax import lax
from jax.experimental import pallas as pl
from jax.experimental.pallas import tpu as pltpu
from jax.sharding import Mesh, PartitionSpec as P

HEAD_DIM = 64
HEADS_DEV = 3
EPS = 1e-06
NEG = -1e30
CTX = ("z", "y", "xh", "core")
CHIPS = ("z", "y", "xh")
F32 = jnp.float32
BF16 = jnp.bfloat16
NT = (((1,), (1,)), ((), ()))
VMEM_LIMIT = 50 * 1024 * 1024
OFFSETS = (0, -1, 1, 2)


def shifted(x, axis, step):
    n = lax.axis_size(axis)
    return lax.ppermute(x, axis, [(i, (i + step) % n) for i in range(n)])


def ring_blocks(x, axis):
    return [x, shifted(x, axis, 1), shifted(x, axis, -1), shifted(x, axis, 2)]


def gather_relative(x, first, second):
    both = jnp.concatenate([x, shifted(x, "xh", 1)], axis=0)
    eight = jnp.concatenate(ring_blocks(both, first), axis=0)
    return ring_blocks(eight, second)


def relative_order(first, second, core_at):
    place = {a: lax.axis_index(a) for a in CHIPS}
    core = lax.axis_index("core")
    order = []
    for second_step in OFFSETS:
        for first_step in OFFSETS:
            for xh_step in (0, 1):
                at = dict(place)
                at[first] = (at[first] + first_step) % 4
                at[second] = (at[second] + second_step) % 4
                at["xh"] = (at["xh"] + xh_step) % 2
                order.append(((at["z"] * 4 + at["y"]) * 2 + at["xh"]) * 2 + (core + core_at) % 2)
    return jnp.stack(order)


def ring_ordered(x, axis):
    own, before, after, far = ring_blocks(x, axis)
    stacked = jnp.stack([own, after, far, before] * 2)
    return lax.dynamic_slice_in_dim(stacked, 4 - lax.axis_index(axis), 4, 0)


def pair_ordered(own, other, axis):
    first = lax.axis_index(axis) == 0
    return jnp.stack([jnp.where(first, own, other), jnp.where(first, other, own)])


def gather_ordered(x, z_first):
    pair = pair_ordered(x, shifted(x, "xh", 1), "xh")
    if z_first:
        whole = jnp.swapaxes(ring_ordered(ring_ordered(pair, "z"), "y"), 0, 1)
    else:
        whole = ring_ordered(ring_ordered(pair, "y"), "z")
    return whole.reshape(-1, *x.shape[1:])


def ring_summed(x, axis, dim):
    at = lax.axis_index(axis)

    def block(step):
        return lax.dynamic_index_in_dim(x, (at + step) % 4, dim, keepdims=False)

    total = block(0).astype(F32)
    for step in (1, -1, 2):
        total = total + shifted(block(step).astype(BF16), axis, step).astype(F32)
    return total


def scatter_summed(x, z_first):
    parts = x.reshape(4, 4, 2, -1, x.shape[-1])
    if z_first:
        parts = ring_summed(ring_summed(parts, "z", 0), "y", 0)
    else:
        parts = ring_summed(ring_summed(parts, "y", 1), "z", 0)
    at = lax.axis_index("xh")
    own = lax.dynamic_index_in_dim(parts, at, 0, keepdims=False)
    theirs = lax.dynamic_index_in_dim(parts, 1 - at, 0, keepdims=False)
    return own + shifted(theirs.astype(BF16), "xh", 1).astype(F32)


def team_sum(partial):
    rows = partial.shape[0] // 2
    near = partial[:rows] + shifted(partial[rows:].astype(BF16), "core", 1).astype(F32)
    low = lax.optimization_barrier(near.astype(BF16))
    return low.astype(F32) + shifted(low, "heads", 1).astype(F32)


def chip_tokens(x):
    return jnp.concatenate([x, shifted(x, "core", 1)], axis=0)


def layer_norm(residual, gain_row, shift_row):
    centred = residual - jnp.mean(residual, axis=-1, keepdims=True)
    inverse = lax.rsqrt(jnp.mean(centred * centred, axis=-1, keepdims=True) + EPS)
    normed = centred * inverse
    return (normed * gain_row + shift_row, normed, inverse)


def norm_back(incoming, normed, inverse, gain_row):
    scaled = incoming * gain_row
    projected = (
        scaled
        - jnp.mean(scaled, axis=-1, keepdims=True)
        - normed * jnp.mean(scaled * normed, axis=-1, keepdims=True)
    )
    return (inverse * projected, jnp.sum(incoming * normed, axis=0), jnp.sum(incoming, axis=0))


def exact_gelu(pre_act):
    return jax.nn.gelu(pre_act, approximate=False)


def pieces_of(column):
    high = column.astype(BF16).astype(F32)
    middle = (column - high).astype(BF16).astype(F32)
    return high, middle, column - high - middle


def head_columns(h):
    return slice(h * HEAD_DIM, (h + 1) * HEAD_DIM)


def head_block(h):
    return slice(h * 128, (h + 1) * 128)


def diagonal_scores(q_ref, kv_ref, h):
    product = q_ref[h].astype(F32) * kv_ref[:, head_block(h)].astype(F32)
    return jnp.sum(product, axis=1, keepdims=True)


def copies_in(sources, buffer, sems):
    copies = [
        pltpu.make_async_copy(source, buffer.at[j], sems.at[j]) for j, source in enumerate(sources)
    ]
    for copy in copies:
        copy.start()


def attend_kernel(q_ref, own_ref, tags_ref, seg_ref, tag_ref, *rest):
    blocks, (out_ref, stat_ref, sent_ref, buffer, top, total, acc, sems) = rest[:8], rest[8:]
    copies_in(blocks, buffer, sems)
    rows = q_ref.shape[1]
    padded = tag_ref[...] < 0
    seg_wide = jnp.broadcast_to(seg_ref[...], (rows, 128))
    for h in range(HEADS_DEV):
        diagonal = diagonal_scores(q_ref, own_ref, h)
        top[h] = jnp.broadcast_to(jnp.where(padded, diagonal, NEG), (rows, 128))
        lane = lax.broadcasted_iota(jnp.int32, (rows, 128), 1)
        total[h] = jnp.where((lane == 0) & padded, 1.0, 0.0)
        acc[h] = jnp.where(padded, own_ref[:, head_block(h)].astype(F32), 0.0)

    def step(j, carry):
        pltpu.make_async_copy(blocks[0], buffer.at[j], sems.at[j]).wait()
        tags = tags_ref[pl.ds(j, 1), :]
        keys = tags.shape[1]
        allowed = jnp.tile(seg_wide, (1, keys // 128)) == tags
        for h in range(HEADS_DEV):
            kv = buffer[j, :, head_block(h)]
            scores = lax.dot_general(q_ref[h], kv, NT, preferred_element_type=F32)
            scores = jnp.where(allowed, scores, NEG)
            before = top[h]
            now = jnp.maximum(before, jnp.max(scores, axis=1, keepdims=True))
            weights = jnp.exp(scores - jnp.tile(now, (1, keys // 128)))
            fade = jnp.exp(before - now)
            sums = weights[:, :128]
            for k in range(1, keys // 128):
                sums = sums + weights[:, k * 128 : (k + 1) * 128]
            total[h] = total[h] * fade + sums
            acc[h] = acc[h] * fade + jnp.dot(weights.astype(BF16), kv, preferred_element_type=F32)
            top[h] = now
        return carry

    lax.fori_loop(0, 8, step, 0)
    lane = lax.broadcasted_iota(jnp.int32, (rows, HEAD_DIM), 1)
    seg = seg_ref[...]
    extra = jnp.where(lane == 12, 1.0, 0.0)
    for s in range(3):
        extra = extra + jnp.where((lane == 9 + s) & (seg != s), 1.0, 0.0)
    outs, queries = [], []
    for h in range(HEADS_DEV):
        sums = jnp.sum(total[h], axis=1, keepdims=True)
        outs.append((acc[h] / sums)[:, HEAD_DIM:])
        stat = top[h] + jnp.log(sums)
        stat_ref[h] = stat
        for i, piece in enumerate(pieces_of(stat[:, :1])):
            extra = extra + jnp.where(lane == 3 * h + i, piece, 0.0)
        queries.append(q_ref[h][:, :HEAD_DIM].astype(F32))
    out_ref[...] = jnp.concatenate(outs, axis=1)
    sent_ref[...] = jnp.concatenate(queries + [extra], axis=1).astype(BF16)


def vmem_specs(n):
    return [pl.BlockSpec(memory_space=pltpu.VMEM)] * n


def any_specs(n):
    return [pl.BlockSpec(memory_space=pl.ANY)] * n


def attend(q_heads, kv_own, tags, seg, tag, blocks):
    rows = kv_own.shape[0]
    keys, width = blocks[0].shape
    pairs = rows * keys * 8 * HEADS_DEV
    return pl.pallas_call(
        attend_kernel,
        out_shape=(
            jax.ShapeDtypeStruct((rows, HEADS_DEV * HEAD_DIM), F32),
            jax.ShapeDtypeStruct((HEADS_DEV, rows, 128), F32),
            jax.ShapeDtypeStruct((rows, 256), BF16),
        ),
        in_specs=vmem_specs(5) + any_specs(8),
        out_specs=tuple(vmem_specs(3)),
        scratch_shapes=[
            pltpu.VMEM((8, keys, width), BF16),
            pltpu.VMEM((HEADS_DEV, rows, 128), F32),
            pltpu.VMEM((HEADS_DEV, rows, 128), F32),
            pltpu.VMEM((HEADS_DEV, rows, 128), F32),
            pltpu.SemaphoreType.DMA((8,)),
        ],
        compiler_params=pltpu.CompilerParams(vmem_limit_bytes=VMEM_LIMIT),
        cost_estimate=pl.CostEstimate(
            flops=pairs * 512, bytes_accessed=8 * keys * width * 2, transcendentals=pairs
        ),
        name="attend",
    )(q_heads, kv_own, tags, seg, tag, *blocks)


def query_back_kernel(q_ref, g_ref, own_ref, tags_ref, seg_ref, tag_ref, stat_ref, delta_ref, *rest):
    blocks, (dq_ref, dkv_ref, buffer, acc, sems) = rest[:8], rest[8:]
    copies_in(blocks, buffer, sems)
    rows = q_ref.shape[1]
    seg_wide = jnp.broadcast_to(seg_ref[...], (rows, 128))
    padded = tag_ref[...] < 0
    for h in range(HEADS_DEV):
        own = own_ref[:, head_block(h)].astype(F32)
        prob = jnp.exp(diagonal_scores(q_ref, own_ref, h) - stat_ref[h][:, :1])
        prob = jnp.where(padded, prob, 0.0)
        grad = diagonal_scores(g_ref, own_ref, h) - delta_ref[h][:, :1]
        score = (prob * grad).astype(BF16).astype(F32)
        acc[h] = score * own
        dkv_ref[:, head_block(h)] = score * q_ref[h].astype(F32) + prob.astype(BF16).astype(
            F32
        ) * g_ref[h].astype(F32)

    def step(j, carry):
        pltpu.make_async_copy(blocks[0], buffer.at[j], sems.at[j]).wait()
        tags = tags_ref[pl.ds(j, 1), :]
        keys = tags.shape[1]
        allowed = jnp.tile(seg_wide, (1, keys // 128)) == tags
        for h in range(HEADS_DEV):
            kv = buffer[j, :, head_block(h)]
            scores = lax.dot_general(q_ref[h], kv, NT, preferred_element_type=F32)
            scores = jnp.where(allowed, scores, NEG)
            probs = jnp.exp(scores - jnp.tile(stat_ref[h], (1, keys // 128)))
            grads = lax.dot_general(g_ref[h], kv, NT, preferred_element_type=F32)
            back = probs * (grads - jnp.tile(delta_ref[h], (1, keys // 128)))
            acc[h] = acc[h] + jnp.dot(back.astype(BF16), kv, preferred_element_type=F32)
        return carry

    lax.fori_loop(0, 8, step, 0)
    dq_ref[...] = (
        jnp.concatenate([acc[h][:, :HEAD_DIM] for h in range(HEADS_DEV)], axis=1)
        * HEAD_DIM ** (-0.5)
    ).astype(BF16)


def query_back(q_heads, g_heads, kv_own, tags, seg, tag, stat, delta, blocks):
    rows = kv_own.shape[0]
    keys, width = blocks[0].shape
    pairs = rows * keys * 8 * HEADS_DEV
    return pl.pallas_call(
        query_back_kernel,
        out_shape=(
            jax.ShapeDtypeStruct((rows, HEADS_DEV * HEAD_DIM), BF16),
            jax.ShapeDtypeStruct((rows, width), F32),
        ),
        in_specs=vmem_specs(8) + any_specs(8),
        out_specs=tuple(vmem_specs(2)),
        scratch_shapes=[
            pltpu.VMEM((8, keys, width), BF16),
            pltpu.VMEM((HEADS_DEV, rows, 128), F32),
            pltpu.SemaphoreType.DMA((8,)),
        ],
        compiler_params=pltpu.CompilerParams(vmem_limit_bytes=VMEM_LIMIT),
        cost_estimate=pl.CostEstimate(
            flops=pairs * 768, bytes_accessed=8 * keys * width * 2, transcendentals=pairs
        ),
        name="query_back",
    )(q_heads, g_heads, kv_own, tags, seg, tag, stat, delta, *blocks)


def grad_rows_kernel(mixed_ref, out_ref, attended_ref, sent_ref, g_ref, delta_ref):
    rows = mixed_ref.shape[0]
    grad = jnp.dot(mixed_ref[...], out_ref[...], preferred_element_type=F32).astype(BF16)
    grad = grad.astype(F32)
    product = grad * attended_ref[...]
    lane = lax.broadcasted_iota(jnp.int32, (rows, HEAD_DIM), 1)
    extra = jnp.zeros((rows, HEAD_DIM), F32)
    zeros = jnp.zeros((rows, HEAD_DIM), BF16)
    for h in range(HEADS_DEV):
        delta = jnp.sum(product[:, head_columns(h)], axis=1, keepdims=True)
        delta_ref[h] = jnp.broadcast_to(delta, (rows, 128))
        for i, piece in enumerate(pieces_of(delta)):
            extra = extra + jnp.where(lane == 3 * h + i, piece, 0.0)
        g_ref[h] = jnp.concatenate([zeros, grad[:, head_columns(h)].astype(BF16)], axis=1)
    sent_ref[...] = jnp.concatenate([grad, extra], axis=1).astype(BF16)


def grad_rows(mixed, w_out, attended):
    rows = mixed.shape[0]
    return pl.pallas_call(
        grad_rows_kernel,
        out_shape=(
            jax.ShapeDtypeStruct((rows, 256), BF16),
            jax.ShapeDtypeStruct((HEADS_DEV, rows, 128), BF16),
            jax.ShapeDtypeStruct((HEADS_DEV, rows, 128), F32),
        ),
        in_specs=vmem_specs(3),
        out_specs=tuple(vmem_specs(3)),
        compiler_params=pltpu.CompilerParams(vmem_limit_bytes=VMEM_LIMIT),
        name="grad_rows",
    )(mixed, w_out, attended)


def key_back_kernel(k_ref, v_ref, diag_ref, *rest):
    q_blocks, g_blocks = rest[:8], rest[8:16]
    dkv_ref, q_buffer, g_buffer, k_acc, v_acc, q_sems, g_sems = rest[16:]
    copies_in(q_blocks, q_buffer, q_sems)
    copies_in(g_blocks, g_buffer, g_sems)
    k_acc[...] = jnp.zeros_like(k_acc)
    v_acc[...] = jnp.zeros_like(v_acc)

    def step(j, carry):
        pltpu.make_async_copy(q_blocks[0], q_buffer.at[j], q_sems.at[j]).wait()
        pltpu.make_async_copy(g_blocks[0], g_buffer.at[j], g_sems.at[j]).wait()
        queries, grads = q_buffer[j], g_buffer[j]
        for h in range(HEADS_DEV):
            scores = lax.dot_general(k_ref[h], queries, NT, preferred_element_type=F32)
            probs = jnp.exp(scores)
            v_acc[h] = v_acc[h] + jnp.dot(probs.astype(BF16), grads, preferred_element_type=F32)
            back = probs * lax.dot_general(v_ref[h], grads, NT, preferred_element_type=F32)
            k_acc[h] = k_acc[h] + jnp.dot(back.astype(BF16), queries, preferred_element_type=F32)
        return carry

    lax.fori_loop(0, 8, step, 0)
    parts = []
    for h in range(HEADS_DEV):
        parts += [k_acc[h][:, head_columns(h)], v_acc[h][:, head_columns(h)]]
    dkv_ref[...] = (jnp.concatenate(parts, axis=1) + diag_ref[...]).astype(BF16)


def key_back(k_heads, v_heads, diagonal, q_blocks, g_blocks):
    rows = k_heads.shape[1]
    queries, width = q_blocks[0].shape
    pairs = rows * queries * 8 * HEADS_DEV
    return pl.pallas_call(
        key_back_kernel,
        out_shape=jax.ShapeDtypeStruct(diagonal.shape, BF16),
        in_specs=vmem_specs(3) + any_specs(16),
        out_specs=vmem_specs(1)[0],
        scratch_shapes=[
            pltpu.VMEM((8, queries, width), BF16),
            pltpu.VMEM((8, queries, width), BF16),
            pltpu.VMEM((HEADS_DEV, rows, width), F32),
            pltpu.VMEM((HEADS_DEV, rows, width), F32),
            pltpu.SemaphoreType.DMA((8,)),
            pltpu.SemaphoreType.DMA((8,)),
        ],
        compiler_params=pltpu.CompilerParams(vmem_limit_bytes=VMEM_LIMIT),
        cost_estimate=pl.CostEstimate(
            flops=pairs * 2048, bytes_accessed=16 * queries * width * 2, transcendentals=pairs
        ),
        name="key_back",
    )(k_heads, v_heads, diagonal, *q_blocks, *g_blocks)


def dot(a, b):
    return jnp.dot(a, b, preferred_element_type=F32)


def dot_nt(a, b):
    return lax.dot_general(a, b, NT, preferred_element_type=F32)


def dot_tn(a, b):
    return lax.dot_general(a, b, (((0,), (0,)), ((), ())), preferred_element_type=F32)


def core_half(x, axis, at):
    size = x.shape[axis] // 2
    return lax.dynamic_slice_in_dim(x, at * size, size, axis)


def interleaved(k, v):
    shape = (*k.shape[:-1], -1, HEAD_DIM)
    return jnp.stack([k.reshape(shape), v.reshape(shape)], axis=-2).reshape(*k.shape[:-1], -1)


def per_device(
    hidden,
    w_qkv,
    w_out,
    b_qv,
    w_up,
    w_down,
    b_up,
    norm_gains,
    norm_shifts,
    segments,
    lengths,
    cotangent,
):
    core = lax.axis_index("core")
    heads_at = lax.axis_index("heads")
    own_ctx = ((lax.axis_index("z") * 4 + lax.axis_index("y")) * 2 + lax.axis_index("xh")) * 2 + core
    tok = hidden.shape[0]
    rows = w_up.shape[0]
    feat = HEADS_DEV * HEAD_DIM
    hidden_units = w_up.shape[1] // 2

    hid = chip_tokens(hidden)
    out_turned, down_turned = w_out.T, w_down.T
    segs_low = segments.astype(BF16).reshape(2, tok // 2)

    def packed(at):
        q, k, v = (core_half(w_qkv[i], 1, at) for i in range(3))
        tail = jnp.pad(segs_low, ((0, rows - 2), (0, 0)))
        urgent = jnp.concatenate([interleaved(k, v), q, tail], axis=1)
        later = [core_half(w, 1, at) for w in (out_turned, w_up, down_turned)]
        return urgent, jnp.concatenate(later, axis=1)

    mine, theirs = packed(core), packed(1 - core)
    urgent = pair_ordered(mine[0], shifted(theirs[0], "core", 1), "core").reshape(2 * rows, -1)
    later = pair_ordered(mine[1], shifted(theirs[1], "core", 1), "core").reshape(2 * rows, -1)
    kv_cols = 2 * feat
    w_kv = gather_ordered(urgent[:, :kv_cols], True)
    w_q_tail = gather_ordered(urgent[:, kv_cols:], False)
    w_q = w_q_tail[:, :feat]
    seg_all = w_q_tail[:, feat:].reshape(-1, 2, rows, tok // 2)[:, :, :2].reshape(-1, tok)
    seg_all = seg_all.astype(jnp.int32)
    rest = lax.all_gather(later, CHIPS, axis=0, tiled=True)
    w_out_t = rest[:, :feat]
    w_up_all = rest[:, feat : feat + hidden_units]
    w_down_t = rest[:, feat + hidden_units :]

    bias = b_qv.astype(F32)
    q_bias, v_bias = core_half(bias[0], 0, core), core_half(bias[1], 0, core)
    kv_own = (dot(hid, w_kv) + interleaved(jnp.zeros_like(v_bias), v_bias)).astype(BF16)
    queries = ((dot(hid, w_q) + q_bias).astype(BF16) * HEAD_DIM ** (-0.5)).astype(BF16)
    q_heads = jnp.pad(
        jnp.swapaxes(queries.reshape(2 * tok, HEADS_DEV, HEAD_DIM), 0, 1),
        ((0, 0), (0, 0), (0, HEAD_DIM)),
    )

    starts = [jnp.sum((seg_all < s).astype(jnp.int32)) for s in range(3)]
    places = jnp.arange(seg_all.size, dtype=jnp.int32).reshape(seg_all.shape)
    run_end = jnp.zeros_like(seg_all)
    for s in range(3):
        run_end = jnp.where(seg_all == s, starts[s] + lengths[s], run_end)
    tag_all = jnp.where(places < run_end, seg_all, -1).astype(F32)
    order = jnp.concatenate([relative_order("z", "y", 0), relative_order("y", "z", 1)])
    tags = jnp.take(tag_all, order, axis=0).reshape(8, -1)
    both = jnp.stack([own_ctx, own_ctx + 1 - 2 * core])
    tag_own = jnp.take(tag_all, both, axis=0).reshape(-1, 1)
    seg_own = jnp.take(seg_all, both, axis=0).astype(F32).reshape(-1, 1)

    kv_blocks = gather_relative(kv_own[:tok], "z", "y") + gather_relative(kv_own[tok:], "y", "z")
    attended, stat, q_sent = attend(q_heads, kv_own, tags, seg_own, tag_own, kv_blocks)
    attended_low = attended.astype(BF16)
    q_blocks = gather_relative(q_sent[:tok], "z", "y") + gather_relative(q_sent[tok:], "y", "z")

    gain_rows = norm_gains.astype(F32)
    shifts = norm_shifts.astype(F32)
    attn_mixed = team_sum(dot_nt(attended_low, w_out_t))
    first_out, normed_one, inverse_one = layer_norm(
        hidden.astype(F32) + attn_mixed + shifts[0], gain_rows[0], shifts[1]
    )
    first_low = chip_tokens(first_out.astype(BF16))
    up_bias = core_half(b_up, 0, core).astype(F32)
    up_proj = dot(first_low, w_up_all) + up_bias
    activated = exact_gelu(up_proj).astype(BF16)
    second = team_sum(dot_nt(activated, w_down_t))
    output, normed_two, inverse_two = layer_norm(
        first_out + second + shifts[2], gain_rows[1], shifts[3]
    )
    resid_two, gain_two_grad, beta_two_grad = norm_back(
        cotangent.astype(F32), normed_two, inverse_two, gain_rows[1]
    )
    branch_low = chip_tokens(resid_two.astype(BF16))
    act_grad = dot(branch_low, w_down_t)
    up_low = jax.vjp(exact_gelu, up_proj)[1](act_grad)[0].astype(BF16)
    first_grad = resid_two + team_sum(dot_nt(up_low, w_up_all))
    down_grad = dot_tn(branch_low, activated)
    up_grad = dot_tn(first_low, up_low)
    upbias_grad = jnp.sum(up_low.astype(F32), axis=0)
    resid_one, gain_one_grad, beta_one_grad = norm_back(
        first_grad, normed_one, inverse_one, gain_rows[0]
    )
    mixed_low = chip_tokens(resid_one.astype(BF16))
    g_sent, g_heads, delta = grad_rows(mixed_low, w_out_t, attended)
    g_blocks = gather_relative(g_sent[:tok], "z", "y") + gather_relative(g_sent[tok:], "y", "z")
    out_grad = dot_tn(mixed_low, attended_low)
    up_done = scatter_summed(up_grad, True)
    down_done = scatter_summed(jnp.concatenate([down_grad, out_grad], axis=1), False)

    dq, diagonal = query_back(
        q_heads, g_heads, kv_own, tags, seg_own, tag_own, stat, delta, kv_blocks
    )
    lane = jnp.arange(256, dtype=jnp.int32)
    split = kv_own.reshape(2 * tok, HEADS_DEV, 2, HEAD_DIM)
    extras = jnp.where(
        (lane >= feat + 9) & (lane < feat + 12),
        jnp.where(tag_own == (lane - feat - 9).astype(F32), NEG, 0.0),
        jnp.where((lane == feat + 12) & (tag_own < 0), NEG, 0.0),
    )

    def spread_heads(x, more):
        wide = jnp.pad(x.reshape(2 * tok, feat).astype(F32), ((0, 0), (0, 256 - feat)))
        made = []
        for h in range(HEADS_DEV):
            in_head = (lane >= h * HEAD_DIM) & (lane < (h + 1) * HEAD_DIM)
            in_stat = (lane >= feat + 3 * h) & (lane < feat + 3 * h + 3)
            made.append(jnp.where(in_head, wide, jnp.where(in_stat, -1.0, more)))
        return jnp.stack(made).astype(BF16)

    k_heads = spread_heads(split[:, :, 0], extras)
    v_heads = spread_heads(split[:, :, 1], jnp.zeros_like(extras))
    dkv = key_back(k_heads, v_heads, diagonal, q_blocks, g_blocks)

    hidden_grad = resid_one + team_sum(dot_nt(dkv, w_kv) + dot_nt(dq, w_q))

    def placed_half(x):
        zero = jnp.zeros_like(x)
        return jnp.concatenate(
            [jnp.where(core == 0, x, zero), jnp.where(core == 0, zero, x)], axis=-1
        )

    dv = dkv.reshape(2 * tok, HEADS_DEV, 2, HEAD_DIM)[:, :, 1].reshape(2 * tok, feat)
    qv_grad = jnp.stack([jnp.sum(dq.astype(F32), axis=0), jnp.sum(dv.astype(F32), axis=0)])
    vectors = jnp.stack(
        [
            gain_one_grad,
            gain_two_grad,
            jnp.sum(resid_one, axis=0),
            beta_one_grad,
            jnp.sum(resid_two, axis=0),
            beta_two_grad,
        ]
    )

    def by_owner(x):
        return jnp.swapaxes(x.reshape(x.shape[0], 64, -1), 0, 1).reshape(64, -1)

    small = jnp.concatenate(
        [by_owner(placed_half(qv_grad)), by_owner(placed_half(upbias_grad)[None]), by_owner(vectors)],
        axis=1,
    )
    small = jnp.pad(small, ((0, 0), (0, 128 - small.shape[1]))).reshape(64, 2, 64)
    small = jnp.pad(small, ((0, 0), (0, rows - 2), (0, 0))).reshape(64 * rows, 64)
    kv_done = scatter_summed(dot_tn(hid, dkv), True)
    q_done = scatter_summed(jnp.concatenate([dot_tn(hid, dq), small], axis=1), False)

    done = jnp.concatenate([kv_done, q_done, up_done, down_done], axis=1)
    own_rows = core_half(done, 0, core)
    got = shifted(core_half(done, 0, 1 - core), "core", 1)
    low = jnp.where(core == 0, own_rows, got)
    high = jnp.where(core == 0, got, own_rows)

    def columns(start, size):
        return jnp.concatenate(
            [low[:, start : start + size], high[:, start : start + size]], axis=1
        )

    kv_pairs = columns(0, kv_cols).reshape(rows, 2 * HEADS_DEV, 2, HEAD_DIM)
    k_cols = kv_pairs[:, :, 0].reshape(rows, -1)
    v_cols = kv_pairs[:, :, 1].reshape(rows, -1)
    q_cols = columns(kv_cols, feat)
    at = kv_cols + feat
    tail = (own_rows + got)[:2, at : at + 64].reshape(-1)
    at += 64
    up_cols = columns(at, hidden_units)
    down_cols = columns(at + hidden_units, hidden_units)
    out_cols = columns(at + 2 * hidden_units, feat)
    qv_out = tail[:12].reshape(2, 6)
    bias_out = tail[12:36]
    vec_out = tail[36:108].reshape(6, 2, 6)
    vec_out = lax.dynamic_index_in_dim(vec_out, heads_at, 1, keepdims=False)
    return (
        output.astype(BF16),
        hidden_grad,
        jnp.stack([q_cols, k_cols, v_cols]),
        out_cols.T,
        qv_out,
        up_cols,
        down_cols.T,
        bias_out,
        vec_out[:2],
        vec_out[2:],
    )


def solution(mesh):
    fine = Mesh(mesh.devices.reshape(4, 4, 2, 2, 2), ("z", "y", "xh", "core", "heads"))
    return jax.shard_map(
        per_device,
        mesh=fine,
        in_specs=(
            P(CTX, None),
            P(None, CTX, "heads"),
            P("heads", CTX),
            P(None, "heads"),
            P(CTX, "heads"),
            P("heads", CTX),
            P("heads"),
            P(),
            P(),
            P(CTX),
            P(),
            P(CTX, None),
        ),
        out_specs=(
            P(CTX, None),
            P(CTX, None),
            P(None, CTX, "heads"),
            P("heads", CTX),
            P(None, ("heads", *CTX)),
            P(CTX, "heads"),
            P("heads", CTX),
            P(("heads", *CTX)),
            P(None, (*CTX, "heads")),
            P(None, (*CTX, "heads")),
        ),
        check_vma=False,
    )
```

time: 1410 us -> 469 us (0.33); the launches traced: 1380 us -> 459 us
  blocking collectives: 538 us -> 0 us
  waiting for transfers between devices: 406 us -> 150 us
  matrix products: 101 us -> 20 us
  local copies, waits for them, and re-layouts: 111 us -> 52.5 us
  Pallas kernels: 0 us -> 44.9 us
  other arithmetic: 44.6 us -> 21.4 us
  starting transfers between devices: 165 us -> 150 us
    unnamed x2 -> x0, blocking collectives: 523 us -> none
    reduce_scatter x1 -> x0, waiting for transfers between devices: 213 us -> none  [in_one_piece(): lax.psum_scatter(both, axis, scatter_dimension=dim, tiled=True)]
    all_gather x2 -> x1, waiting for transfers between devices: 179 us -> 0.01 us  [per_device(): rest = lax.all_gather(later, CHIPS, axis=0, tiled=True)]
    ppermute x0 -> x99, waiting for transfers between devices: none -> 150 us  [shifted(): return lax.ppermute(x, axis, [(i, (i + step) % n) for i in range(n)])]
    ppermute x0 -> x99, starting transfers between devices: none -> 150 us  [shifted(): return lax.ppermute(x, axis, [(i, (i + step) % n) for i in range(n)])]
    unnamed x49 -> x0, starting transfers between devices: 146 us -> none
    dot_general x24 -> x14, matrix products: 101 us -> 20 us  [the longest x4 6.87 us: dot(): return jnp.dot(a, b, preferred_element_type=F32)]
    unnamed x129 -> x156, local copies, waits for them, and re-layouts: 85.5 us -> 20.4 us
  transfers between devices with their start and end apart: 55 -> 100, of which waited for: 5 -> 38; matrix products, arithmetic and copies ran while one was open for 23% -> 16% of each run, Pallas kernels for 0% -> 3%
where the time goes in v1:
time: 469 us; the launch traced here: 459 us
  starting transfers between devices  150 us (32%)
  waiting for transfers between devices  150 us (32%)
  local copies, waits for them, and re-layouts  52.5 us (11%)
  Pallas kernels  44.9 us (10%)
  other arithmetic  21.4 us (5%)
  between operations  20.3 us (4%)
  matrix products  20 us (4%)
    ppermute x99, waiting for transfers between devices, shifted(): return lax.ppermute(x, axis, [(i, (i + step) % n) for i in range(n)])  150 us
    ppermute x99, starting transfers between devices, shifted(): return lax.ppermute(x, axis, [(i, (i + step) % n) for i in range(n)])  150 us
    unnamed x156, local copies, waits for them, and re-layouts  20.4 us
    pallas_call x1, Pallas kernels, key_back(): pl.pallas_call(key_back_kernel, out_shape=jax.ShapeDtypeStruct(diagonal.s...  17.1 us
    pallas_call x1, Pallas kernels, attend(): pl.pallas_call(attend_kernel, out_shape=(jax.ShapeDtypeStruct((rows, HEAD...  14 us
    pallas_call x1, Pallas kernels, query_back(): pl.pallas_call(query_back_kernel, out_shape=(jax.ShapeDtypeStruct((rows,...  12.9 us
  transfers between devices with their start and end apart: 100, of which 38 were waited for; matrix products, arithmetic and copies ran while one was open for 16% of the time, Pallas kernels for 3%

profile of v1, /device:TPU:1, one launch (start us, length us, event | category | flops | bytes accessed | tf_op | source)
XLA Modules:
  0.0 459.4 jit_solution(7940901513496101370)
XLA Ops:
  18.2 2.9 collective-permute-start.2
  22.3 2.9 collective-permute-start.3
  27.2 3.8 collective-permute-start.10
  67.5 4.3 collective-permute-done.18
  71.8 3.1 collective-permute-done.19
  81.9 17.8 %collective-permute-done.24 = bf16[256,384]{1,0:T(8,128)(2,1)S(1)} collective-permute-done((bf16[256,384]{1,0:T(8,128)(2,1)S(1)}, bf16[256,384]{1,0:T(8,128)(2,1)S(1)}, u32[]{:S(2)}, u32[]{:S(2)}) %collective-permute-start.24) | collective-permute-done | bytes 196640 | tf_op jit(solution)/shard_map/ppermute | solution.py:23
  106.0 3.5 collective-permute-done.21.rest_2_
  109.4 9.4 %collective-permute-done.22.rest_3_ = bf16[1024,384]{1,0:T(8,128)(2,1)} collective-permute-done((bf16[1024,384]{1,0:T(8,128)(2,1)S(1)}, bf16[1024,384]{1,0:T(8,128)(2,1)}, u32[]{:S(2)}, u32[]{:S(2)}) %collective-permute-start.22) | collective-permute-done | bytes 786464 | tf_op jit(solution)/shard_map/ppermute | solution.py:23
  118.8 4.3 collective-permute-done.27.rest_5_
  123.2 14.0 %attend.1 = (f32[256,192]{1,0:T(8,128)S(1)}, f32[3,256,128]{2,1,0:T(8,128)S(1)}, bf16[256,256]{1,0:T(8,128)(2,1)S(1)}) custom-call(bf16[3,256,128]{2,1,0:T(8,128)(2,1)S(1)} %pad.32.q_ref, bf16[256,384]{1,0:T(8,128)(2,1)S(1)} %fusion.own_ref, f32[8,1024]{1,0:T(8,128)S(1)} %bitcast_select_fusion.tags_ref, f32[256,1]{1,0:T(8,128)S(1)} %copy.90.seg_ref, ...), custom_call_target="tpu_custom_call" | custom-call | flops 3221225472 | bytes 6291456 | tf_op jit(solution)/shard_map/attend/pallas_call | solution.py:219
  139.2 21.4 %collective-permute-start.31 = (bf16[128,768]{1,0:T(8,128)(2,1)S(1)}, bf16[128,768]{1,0:T(8,128)(2,1)S(1)}, u32[]{:S(2)}, u32[]{:S(2)}) collective-permute-start(bf16[128,768]{1,0:T(8,128)(2,1)S(1)} %slice.352), channel_id=1, source_target_pairs={{0,2},{2,0},{1,3},{3,1},{4,6},{6,4},{5,7},{7,5},{8,10},{10,8},{9,1... | collective-permute-start | bytes 589832 | tf_op jit(solution)/shard_map/ppermute | solution.py:23
  176.7 3.4 multiply_convert_fusion
  184.9 5.6 %collective-permute-done.35 = bf16[128,768]{1,0:T(8,128)(2,1)S(1)} collective-permute-done((bf16[128,768]{1,0:T(8,128)(2,1)S(1)}, bf16[128,768]{1,0:T(8,128)(2,1)S(1)}, u32[]{:S(2)}, u32[]{:S(2)}) %collective-permute-start.35) | collective-permute-done | bytes 196640 | tf_op jit(solution)/shard_map/ppermute | solution.py:23
  195.4 2.8 convert_reduce_fusion
  208.9 3.1 fusion.51
  212.1 2.8 collective-permute-done.86
  214.8 4.5 collective-permute-done.85
  234.2 2.9 collective-permute-start.39
  247.1 12.9 %query_back.1 = (bf16[256,192]{1,0:T(8,128)(2,1)S(1)}, f32[256,384]{1,0:T(8,128)S(1)}) custom-call(bf16[3,256,128]{2,1,0:T(8,128)(2,1)S(1)} %pad.32.q_ref, bf16[3,256,128]{2,1,0:T(8,128)(2,1)S(1)} %get-tuple-element.19.g_ref, bf16[256,384]{1,0:T(8,128)(2,1)S(1)} %fusion.own_ref, f32[8,1024]{1,0:T(8,128)S(1)} %bitcast_select_fusion.tags_ref, ...), custom_call_target="tpu_custom_call" | custom-call | flops 4831838208 | bytes 6291456 | tf_op jit(solution)/shard_map/query_back/pallas_call | solution.py:286
  268.0 3.6 copy.113
  284.6 3.0 collective-permute-done.57
  297.6 8.9 %collective-permute-done.44.rest_1_ = bf16[1024,256]{1,0:T(8,128)(2,1)S(1)} collective-permute-done((bf16[1024,256]{1,0:T(8,128)(2,1)S(1)}, bf16[1024,256]{1,0:T(8,128)(2,1)S(1)}, u32[]{:S(2)}, u32[]{:S(2)}) %collective-permute-start.44) | collective-permute-done | bytes 524320 | tf_op jit(solution)/shard_map/ppermute | solution.py:23
  308.4 11.3 %collective-permute-done.62 = bf16[256,256]{1,0:T(8,128)(2,1)S(1)} collective-permute-done((bf16[256,256]{1,0:T(8,128)(2,1)S(1)}, bf16[256,256]{1,0:T(8,128)(2,1)S(1)}, u32[]{:S(2)}, u32[]{:S(2)}) %collective-permute-start.62) | collective-permute-done | bytes 131104 | tf_op jit(solution)/shard_map/ppermute | solution.py:23
  326.6 23.1 %collective-permute-done.94 = bf16[2,24,960]{2,1,0:T(8,128)(2,1)S(1)} collective-permute-done((bf16[2,24,960]{2,1,0:T(8,128)(2,1)S(1)}, bf16[2,24,960]{2,1,0:T(8,128)(2,1)S(1)}, u32[]{:S(2)}, u32[]{:S(2)}) %collective-permute-start.94) | collective-permute-done | bytes 92192 | tf_op jit(solution)/shard_map/ppermute | solution.py:23
  350.0 5.0 %collective-permute-done.64 = bf16[256,256]{1,0:T(8,128)(2,1)S(1)} collective-permute-done((bf16[256,256]{1,0:T(8,128)(2,1)S(1)}, bf16[256,256]{1,0:T(8,128)(2,1)S(1)}, u32[]{:S(2)}, u32[]{:S(2)}) %collective-permute-start.64) | collective-permute-done | bytes 131104 | tf_op jit(solution)/shard_map/ppermute | solution.py:23
  363.0 4.8 %collective-permute-done.59.rest_10_ = bf16[1024,256]{1,0:T(8,128)(2,1)} collective-permute-done((bf16[1024,256]{1,0:T(8,128)(2,1)}, bf16[1024,256]{1,0:T(8,128)(2,1)}, u32[]{:S(2)}, u32[]{:S(2)}) %collective-permute-start.59) | collective-permute-done | bytes 524320 | tf_op jit(solution)/shard_map/ppermute | solution.py:23
  372.1 6.3 %collective-permute-done.67.rest_15_ = bf16[1024,256]{1,0:T(8,128)(2,1)} collective-permute-done((bf16[1024,256]{1,0:T(8,128)(2,1)}, bf16[1024,256]{1,0:T(8,128)(2,1)}, u32[]{:S(2)}, u32[]{:S(2)}) %collective-permute-start.67) | collective-permute-done | bytes 524320 | tf_op jit(solution)/shard_map/ppermute | solution.py:23
  379.3 17.1 %key_back.1 = bf16[256,384]{1,0:T(8,128)(2,1)S(1)} custom-call(bf16[3,256,256]{2,1,0:T(8,128)(2,1)S(1)} %pad_maximum_fusion.3.k_ref, bf16[3,256,256]{2,1,0:T(8,128)(2,1)S(1)} %pad_maximum_fusion.4.v_ref, f32[256,384]{1,0:T(8,128)S(1)} %copy-done.12, bf16[1024,256]{1,0:T(8,128)(2,1)S(1)} %copy-done.1, bf16[1024,256]{1,0:T(8,128)(2,1)S(1)} %collective-permute-done.44.rest_1_, ...), custom_call_target="tpu_custom_call" | custom-call | flops 12884901888 | bytes 8388608 | tf_op jit(solution)/shard_map/key_back/pallas_call | solution.py:371
  403.7 7.7 %collective-permute-start.68 = (bf16[128,768]{1,0:T(8,128)(2,1)S(1)}, bf16[128,768]{1,0:T(8,128)(2,1)S(1)}, u32[]{:S(2)}, u32[]{:S(2)}) collective-permute-start(bf16[128,768]{1,0:T(8,128)(2,1)S(1)} %slice.349), channel_id=1, source_target_pairs={{0,2},{2,0},{1,3},{3,1},{4,6},{6,4},{5,7},{7,5},{8,10},{10,8},{9,1... | collective-permute-start | bytes 589832 | tf_op jit(solution)/shard_map/ppermute | solution.py:23
  411.9 2.7 collective-permute-start.81
  424.6 2.9 collective-permute-start.75
  437.9 6.4 %collective-permute-start.98 = (f32[12,2368]{1,0:T(8,128)S(1)}, f32[12,2368]{1,0:T(8,128)S(1)}, u32[]{:S(2)}, u32[]{:S(2)}) collective-permute-start(f32[12,2368]{1,0:T(8,128)S(1)} %constant_dynamic-slice_fusion.1), channel_id=1, source_target_pairs={{0,2},{2,0},{1,3},{3,1},{4,6},{6,4},{5,7},{7,5},{8,10},{10,8},{9,1... | collective-permute-start | bytes 341000 | tf_op jit(solution)/shard_map/ppermute | solution.py:23
  (573 shorter events, 210.9 us)
Async XLA Ops:
  7.2 130.6 %all-gather.2.cloned.1.call-start = ((), (), s32[]{:S(2)}) async-start(), calls=%async_computation | async-start | bytes 2838528 | tf_op jit(solution)/shard_map/all_gather | solution.py:456
  9.8 17.4 %collective-permute-start.30 = (bf16[12,1728]{1,0:T(8,128)(2,1)S(1)}, bf16[12,1728]{1,0:T(8,128)(2,1)S(1)}, u32[]{:S(2)}, u32[]{:S(2)}) collective-permute-start(bf16[12,1728]{1,0:T(8,128)(2,1)S(1)} %concatenate.553), channel_id=1, source_target_pairs={{0,2},{2,0},{1,3},{3,1},{4,6},{6,4},{5,7},{7,5},{8,10},{10,8},{9,1... | collective-permute-start | bytes 124424 | tf_op jit(solution)/shard_map/ppermute | solution.py:23
  11.3 36.6 %collective-permute-start = (bf16[128,768]{1,0:T(8,128)(2,1)}, bf16[128,768]{1,0:T(8,128)(2,1)S(1)}, u32[]{:S(2)}, u32[]{:S(2)}) collective-permute-start(bf16[128,768]{1,0:T(8,128)(2,1)} %param.12), channel_id=1, source_target_pairs={{0,2},{2,0},{1,3},{3,1},{4,6},{6,4},{5,7},{7,5},{8,10},{10,8},{9,1... | collective-permute-start | bytes 589832 | tf_op jit(solution)/shard_map/ppermute | solution.py:23
  75.0 29.4 %collective-permute-start.20 = (bf16[1024,384]{1,0:T(8,128)(2,1)S(1)}, bf16[1024,384]{1,0:T(8,128)(2,1)S(1)}, u32[]{:S(2)}, u32[]{:S(2)}) collective-permute-start(bf16[1024,384]{1,0:T(8,128)(2,1)S(1)} %constant_dynamic-update-slice_fusion.26.rest_0_), channel_id=1, source_target_pairs={{0,8},{8,16},{16,24},{24,0},{1,9},{9,17},{17,25},{25,1},{2,10},{10... | collective-permute-start | bytes 2359304 | tf_op jit(solution)/shard_map/ppermute | solution.py:23
  75.1 24.5 %collective-permute-start.24 = (bf16[256,384]{1,0:T(8,128)(2,1)S(1)}, bf16[256,384]{1,0:T(8,128)(2,1)S(1)}, u32[]{:S(2)}, u32[]{:S(2)}) collective-permute-start(bf16[256,384]{1,0:T(8,128)(2,1)S(1)} %pad_maximum_fusion.12), channel_id=1, source_target_pairs={{0,8},{8,16},{16,24},{24,0},{1,9},{9,17},{17,25},{25,1},{2,10},{10... | collective-permute-start | bytes 589832 | tf_op jit(solution)/shard_map/ppermute | solution.py:23
  77.3 23.0 %collective-permute-start.25 = (bf16[256,384]{1,0:T(8,128)(2,1)S(1)}, bf16[256,384]{1,0:T(8,128)(2,1)S(1)}, u32[]{:S(2)}, u32[]{:S(2)}) collective-permute-start(bf16[256,384]{1,0:T(8,128)(2,1)S(1)} %pad_maximum_fusion.12), channel_id=1, source_target_pairs={{0,24},{8,0},{16,8},{24,16},{1,25},{9,1},{17,9},{25,17},{2,26},{10... | collective-permute-start | bytes 589832 | tf_op jit(solution)/shard_map/ppermute | solution.py:23
  78.9 22.2 %collective-permute-start.26 = (bf16[256,384]{1,0:T(8,128)(2,1)S(1)}, bf16[256,384]{1,0:T(8,128)(2,1)S(1)}, u32[]{:S(2)}, u32[]{:S(2)}) collective-permute-start(bf16[256,384]{1,0:T(8,128)(2,1)S(1)} %pad_maximum_fusion.12), channel_id=1, source_target_pairs={{0,16},{8,24},{16,0},{24,8},{1,17},{9,25},{17,1},{25,9},{2,18},{10... | collective-permute-start | bytes 589832 | tf_op jit(solution)/shard_map/ppermute | solution.py:23
  80.7 28.7 %collective-permute-start.21 = (bf16[1024,384]{1,0:T(8,128)(2,1)S(1)}, bf16[1024,384]{1,0:T(8,128)(2,1)}, u32[]{:S(2)}, u32[]{:S(2)}) collective-permute-start(bf16[1024,384]{1,0:T(8,128)(2,1)S(1)} %constant_dynamic-update-slice_fusion.26.rest_0_), channel_id=1, source_target_pairs={{0,24},{8,0},{16,8},{24,16},{1,25},{9,1},{17,9},{25,17},{2,26},{10... | collective-permute-start | bytes 2359304 | tf_op jit(solution)/shard_map/ppermute | solution.py:23
  99.6 19.2 %collective-permute-start.22 = (bf16[1024,384]{1,0:T(8,128)(2,1)S(1)}, bf16[1024,384]{1,0:T(8,128)(2,1)}, u32[]{:S(2)}, u32[]{:S(2)}) collective-permute-start(bf16[1024,384]{1,0:T(8,128)(2,1)S(1)} %constant_dynamic-update-slice_fusion.26.rest_0_), channel_id=1, source_target_pairs={{0,16},{8,24},{16,0},{24,8},{1,17},{9,25},{17,1},{25,9},{2,18},{10... | collective-permute-start | bytes 2359304 | tf_op jit(solution)/shard_map/ppermute | solution.py:23
  101.7 21.4 %collective-permute-start.27 = (bf16[1024,384]{1,0:T(8,128)(2,1)}, bf16[1024,384]{1,0:T(8,128)(2,1)}, u32[]{:S(2)}, u32[]{:S(2)}) collective-permute-start(bf16[1024,384]{1,0:T(8,128)(2,1)} %constant_dynamic-update-slice_fusion.31.rest_4_), channel_id=1, source_target_pairs={{0,32},{32,64},{64,96},{96,0},{1,33},{33,65},{65,97},{97,1},{2,34}... | collective-permute-start | bytes 2359304 | tf_op jit(solution)/shard_map/ppermute | solution.py:23
  101.7 21.4 %collective-permute-start.28 = (bf16[1024,384]{1,0:T(8,128)(2,1)}, bf16[1024,384]{1,0:T(8,128)(2,1)}, u32[]{:S(2)}, u32[]{:S(2)}) collective-permute-start(bf16[1024,384]{1,0:T(8,128)(2,1)} %constant_dynamic-update-slice_fusion.31.rest_4_), channel_id=1, source_target_pairs={{0,96},{32,0},{64,32},{96,64},{1,97},{33,1},{65,33},{97,65},{2,98}... | collective-permute-start | bytes 2359304 | tf_op jit(solution)/shard_map/ppermute | solution.py:23
  104.4 18.7 %collective-permute-start.29 = (bf16[1024,384]{1,0:T(8,128)(2,1)}, bf16[1024,384]{1,0:T(8,128)(2,1)}, u32[]{:S(2)}, u32[]{:S(2)}) collective-permute-start(bf16[1024,384]{1,0:T(8,128)(2,1)} %constant_dynamic-update-slice_fusion.31.rest_4_), channel_id=1, source_target_pairs={{0,64},{32,96},{64,0},{96,32},{1,65},{33,97},{65,1},{97,33},{2,66}... | collective-permute-start | bytes 2359304 | tf_op jit(solution)/shard_map/ppermute | solution.py:23
  139.2 24.5 %collective-permute-start.31 = (bf16[128,768]{1,0:T(8,128)(2,1)S(1)}, bf16[128,768]{1,0:T(8,128)(2,1)S(1)}, u32[]{:S(2)}, u32[]{:S(2)}) collective-permute-start(bf16[128,768]{1,0:T(8,128)(2,1)S(1)} %slice.352), channel_id=1, source_target_pairs={{0,2},{2,0},{1,3},{3,1},{4,6},{6,4},{5,7},{7,5},{8,10},{10,8},{9,1... | collective-permute-start | bytes 589832 | tf_op jit(solution)/shard_map/ppermute | solution.py:23
  169.1 15.7 %collective-permute-start.43 = (bf16[256,256]{1,0:T(8,128)(2,1)S(1)}, bf16[256,256]{1,0:T(8,128)(2,1)S(1)}, u32[]{:S(2)}, u32[]{:S(2)}) collective-permute-start(bf16[256,256]{1,0:T(8,128)(2,1)S(1)} %pad_maximum_fusion.13), channel_id=1, source_target_pairs={{0,64},{32,96},{64,0},{96,32},{1,65},{33,97},{65,1},{97,33},{2,66}... | collective-permute-start | bytes 393224 | tf_op jit(solution)/shard_map/ppermute | solution.py:23
  174.2 19.8 %collective-permute-start.49 = (bf16[256,256]{1,0:T(8,128)(2,1)S(1)}, bf16[256,256]{1,0:T(8,128)(2,1)S(1)}, u32[]{:S(2)}, u32[]{:S(2)}) collective-permute-start(bf16[256,256]{1,0:T(8,128)(2,1)S(1)} %pad_maximum_fusion.14), channel_id=1, source_target_pairs={{0,24},{8,0},{16,8},{24,16},{1,25},{9,1},{17,9},{25,17},{2,26},{10... | collective-permute-start | bytes 393224 | tf_op jit(solution)/shard_map/ppermute | solution.py:23
  201.3 24.3 %collective-permute-start.37 = (bf16[128,768]{1,0:T(8,128)(2,1)}, bf16[128,768]{1,0:T(8,128)(2,1)}, u32[]{:S(2)}, u32[]{:S(2)}) collective-permute-start(bf16[128,768]{1,0:T(8,128)(2,1)} %slice.350), channel_id=1, source_target_pairs={{0,2},{2,0},{1,3},{3,1},{4,6},{6,4},{5,7},{7,5},{8,10},{10,8},{9,1... | collective-permute-start | bytes 589832 | tf_op jit(solution)/shard_map/ppermute | solution.py:23
  273.4 16.1 %collective-permute-start.93 = (bf16[4,2,24,960]{3,2,1,0:T(8,128)(2,1)S(1)}, bf16[4,2,24,960]{3,2,1,0:T(8,128)(2,1)S(1)}, u32[]{:S(2)}, u32[]{:S(2)}) collective-permute-start(bf16[4,2,24,960]{3,2,1,0:T(8,128)(2,1)S(1)} %get-tuple-element.63), channel_id=1, source_target_pairs={{0,16},{8,24},{16,0},{24,8},{1,17},{9,25},{17,1},{25,9},{2,18},{10... | collective-permute-start | bytes 1105928 | tf_op jit(solution)/shard_map/ppermute | solution.py:23
  275.4 17.4 %collective-permute-start.92 = (bf16[4,2,24,960]{3,2,1,0:T(8,128)(2,1)S(1)}, bf16[4,2,24,960]{3,2,1,0:T(8,128)(2,1)S(1)}, u32[]{:S(2)}, u32[]{:S(2)}) collective-permute-start(bf16[4,2,24,960]{3,2,1,0:T(8,128)(2,1)S(1)} %get-tuple-element.64), channel_id=1, source_target_pairs={{0,24},{8,0},{16,8},{24,16},{1,25},{9,1},{17,9},{25,17},{2,26},{10... | collective-permute-start | bytes 1105928 | tf_op jit(solution)/shard_map/ppermute | solution.py:23
  276.0 18.6 %collective-permute-start.91 = (bf16[4,2,24,960]{3,2,1,0:T(8,128)(2,1)S(1)}, bf16[4,2,24,960]{3,2,1,0:T(8,128)(2,1)S(1)}, u32[]{:S(2)}, u32[]{:S(2)}) collective-permute-start(bf16[4,2,24,960]{3,2,1,0:T(8,128)(2,1)S(1)} %get-tuple-element.62), channel_id=1, source_target_pairs={{0,8},{8,16},{16,24},{24,0},{1,9},{9,17},{17,25},{25,1},{2,10},{10... | collective-permute-start | bytes 1105928 | tf_op jit(solution)/shard_map/ppermute | solution.py:23
  283.6 22.9 %collective-permute-start.44 = (bf16[1024,256]{1,0:T(8,128)(2,1)S(1)}, bf16[1024,256]{1,0:T(8,128)(2,1)S(1)}, u32[]{:S(2)}, u32[]{:S(2)}) collective-permute-start(bf16[1024,256]{1,0:T(8,128)(2,1)S(1)} %copy-done.1), channel_id=1, source_target_pairs={{0,8},{8,16},{16,24},{24,0},{1,9},{9,17},{17,25},{25,1},{2,10},{10... | collective-permute-start | bytes 1572872 | tf_op jit(solution)/shard_map/ppermute | solution.py:23
  287.6 34.8 %collective-permute-start.45 = (bf16[1024,256]{1,0:T(8,128)(2,1)S(1)}, bf16[1024,256]{1,0:T(8,128)(2,1)S(1)}, u32[]{:S(2)}, u32[]{:S(2)}) collective-permute-start(bf16[1024,256]{1,0:T(8,128)(2,1)S(1)} %copy-done.1), channel_id=1, source_target_pairs={{0,24},{8,0},{16,8},{24,16},{1,25},{9,1},{17,9},{25,17},{2,26},{10... | collective-permute-start | bytes 1572872 | tf_op jit(solution)/shard_map/ppermute | solution.py:23
  289.4 33.0 %collective-permute-start.46 = (bf16[1024,256]{1,0:T(8,128)(2,1)S(1)}, bf16[1024,256]{1,0:T(8,128)(2,1)S(1)}, u32[]{:S(2)}, u32[]{:S(2)}) collective-permute-start(bf16[1024,256]{1,0:T(8,128)(2,1)S(1)} %copy-done.1), channel_id=1, source_target_pairs={{0,16},{8,24},{16,0},{24,8},{1,17},{9,25},{17,1},{25,9},{2,18},{10... | collective-permute-start | bytes 1572872 | tf_op jit(solution)/shard_map/ppermute | solution.py:23
  292.9 26.8 %collective-permute-start.62 = (bf16[256,256]{1,0:T(8,128)(2,1)S(1)}, bf16[256,256]{1,0:T(8,128)(2,1)S(1)}, u32[]{:S(2)}, u32[]{:S(2)}) collective-permute-start(bf16[256,256]{1,0:T(8,128)(2,1)S(1)} %pad_maximum_fusion.16), channel_id=1, source_target_pairs={{0,8},{8,16},{16,24},{24,0},{1,9},{9,17},{17,25},{25,1},{2,10},{10... | collective-permute-start | bytes 393224 | tf_op jit(solution)/shard_map/ppermute | solution.py:23
  294.6 30.5 %collective-permute-start.63 = (bf16[256,256]{1,0:T(8,128)(2,1)S(1)}, bf16[256,256]{1,0:T(8,128)(2,1)S(1)}, u32[]{:S(2)}, u32[]{:S(2)}) collective-permute-start(bf16[256,256]{1,0:T(8,128)(2,1)S(1)} %pad_maximum_fusion.16), channel_id=1, source_target_pairs={{0,24},{8,0},{16,8},{24,16},{1,25},{9,1},{17,9},{25,17},{2,26},{10... | collective-permute-start | bytes 393224 | tf_op jit(solution)/shard_map/ppermute | solution.py:23
  306.6 18.6 %collective-permute-start.96 = (bf16[2,24,960]{2,1,0:T(8,128)(2,1)S(1)}, bf16[2,24,960]{2,1,0:T(8,128)(2,1)S(1)}, u32[]{:S(2)}, u32[]{:S(2)}) collective-permute-start(bf16[2,24,960]{2,1,0:T(8,128)(2,1)S(1)} %get-tuple-element.75), channel_id=1, source_target_pairs={{0,64},{32,96},{64,0},{96,32},{1,65},{33,97},{65,1},{97,33},{2,66}... | collective-permute-start | bytes 276488 | tf_op jit(solution)/shard_map/ppermute | solution.py:23
  322.5 34.7 %collective-permute-start.51 = (bf16[1024,256]{1,0:T(8,128)(2,1)S(1)}, bf16[1024,256]{1,0:T(8,128)(2,1)S(1)}, u32[]{:S(2)}, u32[]{:S(2)}) collective-permute-start(bf16[1024,256]{1,0:T(8,128)(2,1)S(1)} %constant_dynamic-update-slice_fusion.41.rest_4_), channel_id=1, source_target_pairs={{0,32},{32,64},{64,96},{96,0},{1,33},{33,65},{65,97},{97,1},{2,34}... | collective-permute-start | bytes 1572872 | tf_op jit(solution)/shard_map/ppermute | solution.py:23
  322.5 34.6 %collective-permute-start.52 = (bf16[1024,256]{1,0:T(8,128)(2,1)S(1)}, bf16[1024,256]{1,0:T(8,128)(2,1)S(1)}, u32[]{:S(2)}, u32[]{:S(2)}) collective-permute-start(bf16[1024,256]{1,0:T(8,128)(2,1)S(1)} %constant_dynamic-update-slice_fusion.41.rest_4_), channel_id=1, source_target_pairs={{0,96},{32,0},{64,32},{96,64},{1,97},{33,1},{65,33},{97,65},{2,98}... | collective-permute-start | bytes 1572872 | tf_op jit(solution)/shard_map/ppermute | solution.py:23
  325.1 32.8 %collective-permute-start.53 = (bf16[1024,256]{1,0:T(8,128)(2,1)S(1)}, bf16[1024,256]{1,0:T(8,128)(2,1)S(1)}, u32[]{:S(2)}, u32[]{:S(2)}) collective-permute-start(bf16[1024,256]{1,0:T(8,128)(2,1)S(1)} %constant_dynamic-update-slice_fusion.41.rest_4_), channel_id=1, source_target_pairs={{0,64},{32,96},{64,0},{96,32},{1,65},{33,97},{65,1},{97,33},{2,66}... | collective-permute-start | bytes 1572872 | tf_op jit(solution)/shard_map/ppermute | solution.py:23
  325.2 35.5 %collective-permute-start.58 = (bf16[1024,256]{1,0:T(8,128)(2,1)}, bf16[1024,256]{1,0:T(8,128)(2,1)S(1)}, u32[]{:S(2)}, u32[]{:S(2)}) collective-permute-start(bf16[1024,256]{1,0:T(8,128)(2,1)} %constant_dynamic-update-slice_fusion.46.rest_8_), channel_id=1, source_target_pairs={{0,8},{8,16},{16,24},{24,0},{1,9},{9,17},{17,25},{25,1},{2,10},{10... | collective-permute-start | bytes 1572872 | tf_op jit(solution)/shard_map/ppermute | solution.py:23
  325.2 24.4 %collective-permute-start.94 = (bf16[2,24,960]{2,1,0:T(8,128)(2,1)S(1)}, bf16[2,24,960]{2,1,0:T(8,128)(2,1)S(1)}, u32[]{:S(2)}, u32[]{:S(2)}) collective-permute-start(bf16[2,24,960]{2,1,0:T(8,128)(2,1)S(1)} %get-tuple-element.74), channel_id=1, source_target_pairs={{0,32},{32,64},{64,96},{96,0},{1,33},{33,65},{65,97},{97,1},{2,34}... | collective-permute-start | bytes 276488 | tf_op jit(solution)/shard_map/ppermute | solution.py:23
  360.7 17.6 %collective-permute-start.67 = (bf16[1024,256]{1,0:T(8,128)(2,1)}, bf16[1024,256]{1,0:T(8,128)(2,1)}, u32[]{:S(2)}, u32[]{:S(2)}) collective-permute-start(bf16[1024,256]{1,0:T(8,128)(2,1)} %constant_dynamic-update-slice_fusion.51.rest_12_), channel_id=1, source_target_pairs={{0,64},{32,96},{64,0},{96,32},{1,65},{33,97},{65,1},{97,33},{2,66}... | collective-permute-start | bytes 1572872 | tf_op jit(solution)/shard_map/ppermute | solution.py:23
  403.7 40.6 %collective-permute-start.68 = (bf16[128,768]{1,0:T(8,128)(2,1)S(1)}, bf16[128,768]{1,0:T(8,128)(2,1)S(1)}, u32[]{:S(2)}, u32[]{:S(2)}) collective-permute-start(bf16[128,768]{1,0:T(8,128)(2,1)S(1)} %slice.349), channel_id=1, source_target_pairs={{0,2},{2,0},{1,3},{3,1},{4,6},{6,4},{5,7},{7,5},{8,10},{10,8},{9,1... | collective-permute-start | bytes 589832 | tf_op jit(solution)/shard_map/ppermute | solution.py:23
  (122 other events, 1090.0 us)
Sparse Core Ops, SparseCore 0:
  31.9 77.2 all-gather.1
